TPU v7x, 512 devices: a whole 4x8x8 slice. The times are simulated.
512 devices in a mesh: layer: 4 (over z_lo, core), row: 4 (over z_hi), col: 32 (over x, y).
Axes of the slice: x: 4, y: 8, z: 8 (z_hi: 4, z_lo: 2; z = z_hi * 2 + z_lo), core: 2. Of those that a mesh axis runs over, the one named last changes fastest.
Arguments:
- sources: float32 [8, 256, 16384], P('layer', 'row', 'col'), may hold values from -14 to 14
- conduct: float32 [8, 256, 16384], P('layer', 'row', 'col'), may hold values from 0.5 to 4
- via_cond: float32 [8, 256, 16384], P('layer', 'row', 'col'), may hold values from 0.5 to 4
- via_map: int32 [8, 256, 16384], P('layer', 'row', 'col'), may hold values 0 or 1
- pad_map: int32 [256, 16384], P('row', 'col'), may hold values 0 or 1
- port_tile: int32 [4, 512], replicated, may hold values from 0 to 16383
- pivots: float32 [4, 512, 512], P(None, 'col'), may hold values from -1 to 2, as said below
- coupling: float32 [3, 512, 512], P(None, 'col'), may hold values from -0.109375 to 0.109375
Outputs:
- drop: float32 [8, 256, 16384], P('layer', 'row', 'col')
- ports: float32 [4, 512], replicated
Inputs may be any that keep to these rules, and one draw needn't show every extreme that they name: `pivots`: each block is symmetric.
All inputs are finite; a program needn't handle non-finite values. No bound on the sum of `via_map` or of `pad_map` on one device may be relied on, other than what follows from the above.
Results may differ from a plain program's by a relative error of at most 0.00023.
Values sent between devices are 32-bit elements; how exact they have to be, the bound alone decides.
A program may use at most 64 MiB of HBM per device.

v0:
```python
import jax
import jax.numpy as jnp
from jax import lax
from jax.sharding import PartitionSpec as P

TILE = 16
PANEL = 512
NPANEL = 4
DEG = 3
ITERS = 2


pad_gain = 8.0
bound_low = 0.1
bound_high = 1.9
restrict_scale = 0.25
prolong_scale = 0.5


def padded(cells, sides, width):
    for axis, dim in sides:
        count = lax.axis_size(axis)
        ends = count - 1
        head = lax.slice_in_dim(cells, 0, width, axis=dim)
        tail = lax.slice_in_dim(cells, cells.shape[dim] - width, cells.shape[dim], axis=dim)
        cells = jnp.concatenate(
            [
                lax.ppermute(tail, axis, [(i, (i + 1) % count) for i in range(ends)]),
                cells,
                lax.ppermute(head, axis, [((i + 1) % count, i) for i in range(ends)]),
            ],
            axis=dim,
        )
    return cells


def shifted(grown):
    return (
        grown[2:, 1:-1, 1:-1],
        grown[:-2, 1:-1, 1:-1],
        grown[1:-1, 2:, 1:-1],
        grown[1:-1, :-2, 1:-1],
        grown[1:-1, 1:-1, 2:],
        grown[1:-1, 1:-1, :-2],
    )


def layer_grow(stack):
    return padded(stack, (("layer", 1), ("row", 2), ("col", 3)), 1)


def apply_grid(field, weights, pad_term, grow):
    grown = grow(field[None])[0]
    result = pad_term * field
    for weight, other in zip(weights, shifted(grown)):
        result = result + weight * (field - other)
    return result


def smooth(resid, weights, pad_term, inverse, grow):
    theta = (bound_high + bound_low) / 2.0
    delta = (bound_high - bound_low) / 2.0
    sigma = theta / delta
    rho = 1.0 / sigma
    change = inverse * resid / theta
    total = change
    for sweep in range(DEG - 1):
        remain = resid - apply_grid(total, weights, pad_term, grow)
        rho_new = 1.0 / (2.0 * sigma - rho)
        change = rho_new * rho * change + 2.0 * rho_new / delta * inverse * remain
        total = total + change
        rho = rho_new
    return total


def shards(sources, conduct, via_cond, via_map, pad_map, port_tile, pivots, coupling):
    highest = lax.Precision.HIGHEST
    layer_count = lax.axis_size("layer")
    vertical = via_cond * via_map.astype(jnp.float32)
    block_rows = sources.shape[1]
    currents, plane_cond, plane_vert = (sources, conduct, vertical)
    row_start = lax.axis_index("row") * block_rows
    top_flag = (lax.axis_index("layer") == layer_count - 1).astype(jnp.float32)
    local_layers, grid_rows, grid_cols = currents.shape
    grown = layer_grow(jnp.stack((plane_cond, plane_vert)))
    near_plane = shifted(grown[0])
    near_vert = shifted(grown[1])
    weights = (
        jnp.sqrt(plane_vert * near_vert[0]),
        jnp.sqrt(plane_vert * near_vert[1]),
        jnp.sqrt(plane_cond * near_plane[2]),
        jnp.sqrt(plane_cond * near_plane[3]),
        jnp.sqrt(plane_cond * near_plane[4]),
        jnp.sqrt(plane_cond * near_plane[5]),
    )
    top_layer = pad_gain * pad_map.astype(jnp.float32) * top_flag
    pad_term = jnp.concatenate(
        (jnp.zeros((local_layers - 1, grid_rows, grid_cols), jnp.float32), top_layer[None]), 0
    )
    diagonal = pad_term
    for weight in weights:
        diagonal = diagonal + weight
    inverse = 1.0 / diagonal
    total_tile_cols = grid_cols * lax.axis_size("col") // TILE
    row_tiles = (row_start + jnp.arange(grid_rows, dtype=jnp.int32)) // TILE
    col_tiles = (lax.axis_index("col") * grid_cols + jnp.arange(grid_cols, dtype=jnp.int32)) // TILE
    flat_tiles = port_tile.reshape(-1)
    row_select = (flat_tiles[:, None] // total_tile_cols == row_tiles[None, :]).astype(jnp.float32)
    col_select = (flat_tiles[:, None] % total_tile_cols == col_tiles[None, :]).astype(jnp.float32)
    share = PANEL // lax.axis_size("col")
    start = lax.axis_index("col") * share
    drop = jnp.zeros((local_layers, grid_rows, grid_cols), jnp.float32)
    ports = jnp.zeros((NPANEL, PANEL), jnp.float32)
    for outer in range(ITERS):
        resid = currents - apply_grid(drop, weights, pad_term, layer_grow)
        plane = jnp.sum(resid, axis=0)
        row_sums = jnp.dot(row_select, plane, precision=highest)
        local_rhs = jnp.sum(row_sums * col_select, axis=1).reshape(NPANEL, PANEL)
        rhs = lax.psum(local_rhs, ("layer", "row", "col")) * (restrict_scale / TILE)
        full = rhs[0]
        forward = [full]
        for section in range(1, NPANEL):
            piece = lax.dynamic_slice_in_dim(rhs[section], start, share) - jnp.dot(
                coupling[section - 1], full, precision=highest
            )
            full = lax.all_gather(piece, "col", axis=0, tiled=True)
            forward.append(full)
        scaled = [
            jnp.dot(pivots[section], forward[section], precision=highest)
            for section in range(NPANEL)
        ]
        results = [None] * NPANEL
        for section in range(NPANEL - 1, -1, -1):
            placed = lax.dynamic_update_slice_in_dim(
                jnp.zeros((PANEL,), jnp.float32), scaled[section], start, 0
            )
            if section < NPANEL - 1:
                later_rows = lax.dynamic_slice_in_dim(results[section + 1], start, share)
                placed = placed - jnp.dot(later_rows, coupling[section], precision=highest)
            results[section] = lax.psum(placed, "col")
        ports = jnp.stack(results)
        weighted_rows = jnp.transpose(row_select) * ports.reshape(-1)[None, :]
        field = jnp.dot(weighted_rows, col_select, precision=highest) * prolong_scale
        lifted = jnp.broadcast_to(field[None], (local_layers, grid_rows, grid_cols))
        drop = drop + lifted + smooth(resid, weights, pad_term, inverse, layer_grow)
    return (drop, ports)


def solution(mesh):
    placed = (
        P("layer", "row", "col"),
        P("layer", "row", "col"),
        P("layer", "row", "col"),
        P("layer", "row", "col"),
        P("row", "col"),
        P(),
        P(None, "col", None),
        P(None, "col", None),
    )
    return jax.shard_map(
        shards,
        mesh=mesh,
        in_specs=placed,
        out_specs=(P("layer", "row", "col"), P()),
        check_vma=False,
    )
```

profile of v0, /device:TPU:1, one launch (start us, length us, event | category | flops | bytes accessed | tf_op | source)
XLA Modules:
  0.0 1376.2 jit_solution(3648968046040628290)
XLA Ops:
  0.7 8.9 collective-permute-start.7
  9.6 1.9 collective-permute-start.6
  13.6 1.9 collective-permute-start
  15.5 2.4 collective-permute-start.1
  20.1 2.4 collective-permute-start.8
  23.9 6.7 collective-permute-start.2
  32.1 3.2 collective-permute-start.10
  37.4 3.4 collective-permute-start.4
  42.8 3.4 collective-permute-done.4
  46.2 3.8 collective-permute-done.5
  52.8 2.6 fusion.4
  55.3 103.9 %psum.70 = f32[4,512]{1,0:T(4,128)S(1)} all-reduce(f32[4,512]{1,0:T(4,128)S(1)} %reshape.145), channel_id=1, replica_groups=mesh['layer'=4,'row'=4,'col'=32] {'layer','row','col'}, use_global_device_ids=true, to_apply=%region_2.3 | all-reduce | flops 2048 | bytes 16384 | tf_op jit(solution)/shard_map/psum | solution.py:119
  159.7 58.9 %all-reduce.1 = f32[512]{0:T(512)S(1)} all-reduce(f32[512]{0:T(512)S(1)} %dynamic-update-slice), channel_id=1, replica_groups=mesh['layer'=4,'row'=4,'col'=32] {'col'}, use_global_device_ids=true, to_apply=%add.1 | all-reduce | flops 512 | bytes 4096
  219.0 55.8 %all-reduce.2 = f32[512]{0:T(512)S(1)} all-reduce(f32[512]{0:T(512)S(1)} %dynamic-update-slice.1), channel_id=1, replica_groups=mesh['layer'=4,'row'=4,'col'=32] {'col'}, use_global_device_ids=true, to_apply=%add.2 | all-reduce | flops 512 | bytes 4096
  275.3 57.6 %all-reduce.3 = f32[512]{0:T(512)S(1)} all-reduce(f32[512]{0:T(512)S(1)} %dynamic-update-slice.2), channel_id=1, replica_groups=mesh['layer'=4,'row'=4,'col'=32] {'col'}, use_global_device_ids=true, to_apply=%add.3 | all-reduce | flops 512 | bytes 4096
  333.2 56.0 %psum.71 = f32[512]{0:T(512)S(1)} all-reduce(f32[512]{0:T(512)S(1)} %dynamic_update_slice.27), channel_id=1, replica_groups=mesh['layer'=4,'row'=4,'col'=32] {'col'}, use_global_device_ids=true, to_apply=%region_3.4 | all-reduce | flops 512 | bytes 4096 | tf_op jit(solution)/shard_map/psum | solution.py:140
  389.6 57.8 %psum.72 = f32[512]{0:T(512)S(1)} all-reduce(f32[512]{0:T(512)S(1)} %sub.193), channel_id=1, replica_groups=mesh['layer'=4,'row'=4,'col'=32] {'col'}, use_global_device_ids=true, to_apply=%region_4.5 | all-reduce | flops 512 | bytes 4096 | tf_op jit(solution)/shard_map/psum | solution.py:140
  447.7 71.4 %collective-permute-start.12 = (f32[1,1,64,512]{3,2,1,0:T(8,128)S(1)}, f32[1,1,64,512]{3,2,1,0:T(8,128)S(1)}, u32[]{:S(2)}, u32[]{:S(2)}) collective-permute-start(f32[1,1,64,512]{3,2,1,0:T(8,128)S(1)} %get-tuple-element.52), channel_id=1, source_target_pairs={{0,128},{128,256},{256,384},{1,129},{129,257},{257,385},{2,130},{1... | collective-permute-start | bytes 393224 | tf_op jit(solution)/shard_map/ppermute | solution.py:28
  519.1 1.9 collective-permute-start.13
  521.3 4.0 collective-permute-done.13
  525.4 4.3 collective-permute-start.14
  531.5 3.4 collective-permute-done.15
  535.1 2.3 collective-permute-start.16
  538.7 57.8 %psum.73 = f32[512]{0:T(512)S(1)} all-reduce(f32[512]{0:T(512)S(1)} %sub.194), channel_id=1, replica_groups=mesh['layer'=4,'row'=4,'col'=32] {'col'}, use_global_device_ids=true, to_apply=%region_5.6 | all-reduce | flops 512 | bytes 4096 | tf_op jit(solution)/shard_map/psum | solution.py:140
  599.1 17.9 %collective-permute-start.18 = (f32[1,1,64,512]{3,2,1,0:T(8,128)}, f32[1,1,64,512]{3,2,1,0:T(8,128)S(1)}, u32[]{:S(2)}, u32[]{:S(2)}) collective-permute-start(f32[1,1,64,512]{3,2,1,0:T(8,128)} %get-tuple-element.50), channel_id=1, source_target_pairs={{0,128},{128,256},{256,384},{1,129},{129,257},{257,385},{2,130},{1... | collective-permute-start | bytes 393224 | tf_op jit(solution)/shard_map/ppermute | solution.py:28
  617.1 1.9 collective-permute-start.19
  619.2 55.7 %psum.74 = f32[1,512]{1,0:T(1,128)S(1)} all-reduce(f32[1,512]{1,0:T(1,128)S(1)} %bitcast.248), channel_id=1, replica_groups=mesh['layer'=4,'row'=4,'col'=32] {'col'}, use_global_device_ids=true, to_apply=%region_6.7 | all-reduce | flops 512 | bytes 4096 | tf_op jit(solution)/shard_map/psum | solution.py:140
  675.0 5.5 collective-permute-start.20
  681.8 3.9 collective-permute-done.21
  685.9 3.6 collective-permute-start.22
  689.5 1.5 collective-permute-start.23
  691.0 2.2 fusion.12
  693.2 2.2 collective-permute-done.23
  696.7 20.4 %collective-permute-start.24 = (f32[1,1,64,512]{3,2,1,0:T(8,128)S(1)}, f32[1,1,64,512]{3,2,1,0:T(8,128)S(1)}, u32[]{:S(2)}, u32[]{:S(2)}) collective-permute-start(f32[1,1,64,512]{3,2,1,0:T(8,128)S(1)} %get-tuple-element.48), channel_id=1, source_target_pairs={{0,128},{128,256},{256,384},{1,129},{129,257},{257,385},{2,130},{1... | collective-permute-start | bytes 393224 | tf_op jit(solution)/shard_map/ppermute | solution.py:28
  717.1 2.1 collective-permute-start.25
  719.2 4.3 collective-permute-done.25
  723.6 2.9 collective-permute-start.26
  727.8 4.0 collective-permute-done.27
  731.9 1.6 collective-permute-start.28
  736.0 4.1 collective-permute-done.29
  740.9 2.5 fusion.5
  743.5 93.6 %psum.75 = f32[4,512]{1,0:T(4,128)S(1)} all-reduce(f32[4,512]{1,0:T(4,128)S(1)} %reshape.146), channel_id=1, replica_groups=mesh['layer'=4,'row'=4,'col'=32] {'layer','row','col'}, use_global_device_ids=true, to_apply=%region_9.10 | all-reduce | flops 2048 | bytes 16384 | tf_op jit(solution)/shard_map/psum | solution.py:119
  837.5 58.2 %all-reduce.4 = f32[512]{0:T(512)S(1)} all-reduce(f32[512]{0:T(512)S(1)} %dynamic-update-slice.3), channel_id=1, replica_groups=mesh['layer'=4,'row'=4,'col'=32] {'col'}, use_global_device_ids=true, to_apply=%add.4 | all-reduce | flops 512 | bytes 4096
  896.1 56.1 %all-reduce.5 = f32[512]{0:T(512)S(1)} all-reduce(f32[512]{0:T(512)S(1)} %dynamic-update-slice.4), channel_id=1, replica_groups=mesh['layer'=4,'row'=4,'col'=32] {'col'}, use_global_device_ids=true, to_apply=%add.5 | all-reduce | flops 512 | bytes 4096
  952.7 57.1 %all-reduce.6 = f32[512]{0:T(512)S(1)} all-reduce(f32[512]{0:T(512)S(1)} %dynamic-update-slice.5), channel_id=1, replica_groups=mesh['layer'=4,'row'=4,'col'=32] {'col'}, use_global_device_ids=true, to_apply=%add.6 | all-reduce | flops 512 | bytes 4096
  1010.2 55.7 %psum.76 = f32[512]{0:T(512)S(1)} all-reduce(f32[512]{0:T(512)S(1)} %dynamic_update_slice.31), channel_id=1, replica_groups=mesh['layer'=4,'row'=4,'col'=32] {'col'}, use_global_device_ids=true, to_apply=%region_10.11 | all-reduce | flops 512 | bytes 4096 | tf_op jit(solution)/shard_map/psum | solution.py:140
  1066.3 57.7 %psum.77 = f32[512]{0:T(512)S(1)} all-reduce(f32[512]{0:T(512)S(1)} %sub.220), channel_id=1, replica_groups=mesh['layer'=4,'row'=4,'col'=32] {'col'}, use_global_device_ids=true, to_apply=%region_11.12 | all-reduce | flops 512 | bytes 4096 | tf_op jit(solution)/shard_map/psum | solution.py:140
  1124.2 73.0 %collective-permute-start.30 = (f32[1,1,64,512]{3,2,1,0:T(8,128)S(1)}, f32[1,1,64,512]{3,2,1,0:T(8,128)S(1)}, u32[]{:S(2)}, u32[]{:S(2)}) collective-permute-start(f32[1,1,64,512]{3,2,1,0:T(8,128)S(1)} %get-tuple-element.46), channel_id=1, source_target_pairs={{0,128},{128,256},{256,384},{1,129},{129,257},{257,385},{2,130},{1... | collective-permute-start | bytes 393224 | tf_op jit(solution)/shard_map/ppermute | solution.py:28
  1197.2 1.9 collective-permute-start.31
  1199.3 4.1 collective-permute-done.31
  1203.5 2.8 collective-permute-start.32
  1208.7 56.4 %psum.78 = f32[512]{0:T(512)S(1)} all-reduce(f32[512]{0:T(512)S(1)} %sub.221), channel_id=1, replica_groups=mesh['layer'=4,'row'=4,'col'=32] {'col'}, use_global_device_ids=true, to_apply=%region_12.13 | all-reduce | flops 512 | bytes 4096 | tf_op jit(solution)/shard_map/psum | solution.py:140
  1265.2 2.7 collective-permute-start.34
  1270.0 4.1 collective-permute-done.35
  1276.6 17.4 %collective-permute-start.36 = (f32[1,1,64,512]{3,2,1,0:T(8,128)}, f32[1,1,64,512]{3,2,1,0:T(8,128)S(1)}, u32[]{:S(2)}, u32[]{:S(2)}) collective-permute-start(f32[1,1,64,512]{3,2,1,0:T(8,128)} %get-tuple-element.44), channel_id=1, source_target_pairs={{0,128},{128,256},{256,384},{1,129},{129,257},{257,385},{2,130},{1... | collective-permute-start | bytes 393224 | tf_op jit(solution)/shard_map/ppermute | solution.py:28
  1294.0 1.9 collective-permute-start.37
  1297.1 55.7 %psum.79 = f32[1,512]{1,0:T(1,128)S(1)} all-reduce(f32[1,512]{1,0:T(1,128)S(1)} %bitcast.249), channel_id=1, replica_groups=mesh['layer'=4,'row'=4,'col'=32] {'col'}, use_global_device_ids=true, to_apply=%region_13.14 | all-reduce | flops 512 | bytes 4096 | tf_op jit(solution)/shard_map/psum | solution.py:140
  1352.9 5.2 collective-permute-start.38
  1358.1 1.5 collective-permute-start.39
  1359.6 2.2 fusion.15
  1361.8 2.8 collective-permute-done.39
  1364.7 3.6 collective-permute-start.40
  1370.4 3.8 collective-permute-done.41
  1374.6 1.7 fusion.88
  (170 shorter events, 42.5 us)
Async XLA Ops:
  0.6 17.4 %copy-start.9 = (s32[4,512]{1,0:T(4,128)S(1)}, s32[4,512]{1,0:T(4,128)}, u32[]{:S(2)}) copy-start(s32[4,512]{1,0:T(4,128)} %param.13) | copy-start | bytes 24580
  0.6 17.4 %copy-start.8 = (s32[64,512]{1,0:T(8,128)S(1)}, s32[64,512]{1,0:T(8,128)}, u32[]{:S(2)}) copy-start(s32[64,512]{1,0:T(8,128)} %param.12) | copy-start | bytes 393220
  0.7 23.2 %copy-start = (f32[2,64,512]{2,1,0:T(8,128)S(1)}, f32[2,64,512]{2,1,0:T(8,128)}, u32[]{:S(2)}) copy-start(f32[2,64,512]{2,1,0:T(8,128)} %param.9) | copy-start | bytes 786436
  0.7 19.4 %collective-permute-start.7 = (f32[1,1,64,512]{3,2,1,0:T(8,128)S(1)}, f32[1,1,64,512]{3,2,1,0:T(8,128)S(1)}, u32[]{:S(2)}, u32[]{:S(2)}) collective-permute-start(f32[1,1,64,512]{3,2,1,0:T(8,128)S(1)} %broadcast.185), channel_id=1, source_target_pairs={{128,0},{256,128},{384,256},{129,1},{257,129},{385,257},{130,2},{2... | collective-permute-start | bytes 393224 | tf_op jit(solution)/shard_map/ppermute | solution.py:30
  9.6 10.4 collective-permute-start.6
  13.6 10.2 collective-permute-start
  15.5 8.3 collective-permute-start.1
  20.1 11.8 collective-permute-start.8
  22.5 9.4 collective-permute-start.9
  23.9 12.7 collective-permute-start.2
  30.6 6.6 collective-permute-start.3
  32.1 10.0 collective-permute-start.10
  35.3 7.1 collective-permute-start.11
  37.4 8.8 collective-permute-start.4
  40.8 9.2 collective-permute-start.5
  50.7 1.0 copy-start.3
  50.7 1.0 copy-start.4
  50.7 1.1 copy-start.5
  52.7 106.6 %copy-start.1 = (f32[3,16,512]{2,1,0:T(8,128)S(1)}, f32[3,16,512]{2,1,0:T(8,128)}, u32[]{:S(2)}) copy-start(f32[3,16,512]{2,1,0:T(8,128)} %param.15) | copy-start | bytes 294916
  52.8 222.1 %copy-start.7 = (f32[4,16,512]{2,1,0:T(8,128)S(1)}, f32[4,16,512]{2,1,0:T(8,128)}, u32[]{:S(2)}) copy-start(f32[4,16,512]{2,1,0:T(8,128)} %param.14) | copy-start | bytes 393220
  447.7 73.7 %collective-permute-start.12 = (f32[1,1,64,512]{3,2,1,0:T(8,128)S(1)}, f32[1,1,64,512]{3,2,1,0:T(8,128)S(1)}, u32[]{:S(2)}, u32[]{:S(2)}) collective-permute-start(f32[1,1,64,512]{3,2,1,0:T(8,128)S(1)} %get-tuple-element.52), channel_id=1, source_target_pairs={{0,128},{128,256},{256,384},{1,129},{129,257},{257,385},{2,130},{1... | collective-permute-start | bytes 393224 | tf_op jit(solution)/shard_map/ppermute | solution.py:28
  519.1 6.3 collective-permute-start.13
  525.4 6.2 collective-permute-start.14
  529.7 5.3 collective-permute-start.15
  535.1 61.4 %collective-permute-start.16 = (f32[1,4,66,1]{3,2,1,0:T(8,128)S(1)}, f32[1,4,66,1]{3,2,1,0:T(8,128)}, u32[]{:S(2)}, u32[]{:S(2)}) collective-permute-start(f32[1,4,66,1]{3,2,1,0:T(8,128)S(1)} %get-tuple-element.26), channel_id=1, source_target_pairs={{0,1},{1,2},{2,3},{3,4},{4,5},{5,6},{6,7},{7,8},{8,9},{9,10},{10,1... | collective-permute-start | bytes 3176 | tf_op jit(solution)/shard_map/ppermute | solution.py:28
  537.4 59.1 %collective-permute-start.17 = (f32[1,4,66,1]{3,2,1,0:T(8,128)S(1)}, f32[1,4,66,1]{3,2,1,0:T(8,128)}, u32[]{:S(2)}, u32[]{:S(2)}) collective-permute-start(f32[1,4,66,1]{3,2,1,0:T(8,128)S(1)} %get-tuple-element.27), channel_id=1, source_target_pairs={{1,0},{2,1},{3,2},{4,3},{5,4},{6,5},{7,6},{8,7},{9,8},{10,9},{11,1... | collective-permute-start | bytes 3176 | tf_op jit(solution)/shard_map/ppermute | solution.py:30
  599.1 75.8 %collective-permute-start.18 = (f32[1,1,64,512]{3,2,1,0:T(8,128)}, f32[1,1,64,512]{3,2,1,0:T(8,128)S(1)}, u32[]{:S(2)}, u32[]{:S(2)}) collective-permute-start(f32[1,1,64,512]{3,2,1,0:T(8,128)} %get-tuple-element.50), channel_id=1, source_target_pairs={{0,128},{128,256},{256,384},{1,129},{129,257},{257,385},{2,130},{1... | collective-permute-start | bytes 393224 | tf_op jit(solution)/shard_map/ppermute | solution.py:28
  617.1 57.9 %collective-permute-start.19 = (f32[1,1,64,512]{3,2,1,0:T(8,128)}, f32[1,1,64,512]{3,2,1,0:T(8,128)S(1)}, u32[]{:S(2)}, u32[]{:S(2)}) collective-permute-start(f32[1,1,64,512]{3,2,1,0:T(8,128)} %get-tuple-element.51), channel_id=1, source_target_pairs={{128,0},{256,128},{384,256},{129,1},{257,129},{385,257},{130,2},{2... | collective-permute-start | bytes 393224 | tf_op jit(solution)/shard_map/ppermute | solution.py:30
  675.0 6.8 collective-permute-start.20
  680.4 5.3 collective-permute-start.21
  685.9 7.3 collective-permute-start.22
  689.5 5.9 collective-permute-start.23
  696.7 22.5 %collective-permute-start.24 = (f32[1,1,64,512]{3,2,1,0:T(8,128)S(1)}, f32[1,1,64,512]{3,2,1,0:T(8,128)S(1)}, u32[]{:S(2)}, u32[]{:S(2)}) collective-permute-start(f32[1,1,64,512]{3,2,1,0:T(8,128)S(1)} %get-tuple-element.48), channel_id=1, source_target_pairs={{0,128},{128,256},{256,384},{1,129},{129,257},{257,385},{2,130},{1... | collective-permute-start | bytes 393224 | tf_op jit(solution)/shard_map/ppermute | solution.py:28
  717.1 23.3 %copy-start.6 = (f32[2,64,512]{2,1,0:T(8,128)S(1)}, f32[2,64,512]{2,1,0:T(8,128)}, u32[]{:S(2)}) copy-start(f32[2,64,512]{2,1,0:T(8,128)} %param.8) | copy-start | bytes 786436
  717.1 6.4 collective-permute-start.25
  723.6 4.2 collective-permute-start.26
  726.4 5.3 collective-permute-start.27
  731.9 4.1 collective-permute-start.28
  733.5 6.6 collective-permute-start.29
  1124.2 75.1 %collective-permute-start.30 = (f32[1,1,64,512]{3,2,1,0:T(8,128)S(1)}, f32[1,1,64,512]{3,2,1,0:T(8,128)S(1)}, u32[]{:S(2)}, u32[]{:S(2)}) collective-permute-start(f32[1,1,64,512]{3,2,1,0:T(8,128)S(1)} %get-tuple-element.46), channel_id=1, source_target_pairs={{0,128},{128,256},{256,384},{1,129},{129,257},{257,385},{2,130},{1... | collective-permute-start | bytes 393224 | tf_op jit(solution)/shard_map/ppermute | solution.py:28
  1197.2 6.3 collective-permute-start.31
  1203.4 66.5 %copy-start.2 = (f32[1,1,64,512]{3,2,1,0:T(8,128)}, f32[1,1,64,512]{3,2,1,0:T(8,128)S(1)}, u32[]{:S(2)}) copy-start(f32[1,1,64,512]{3,2,1,0:T(8,128)S(1)} %collective-permute-done.31) | copy-start | bytes 393220
  1203.5 61.6 %collective-permute-start.32 = (f32[1,4,1,512]{3,2,1,0:T(1,128)S(1)}, f32[1,4,1,512]{3,2,1,0:T(1,128)S(1)}, u32[]{:S(2)}, u32[]{:S(2)}) collective-permute-start(f32[1,4,1,512]{3,2,1,0:T(1,128)S(1)} %get-tuple-element.32), channel_id=1, source_target_pairs={{0,32},{32,64},{64,96},{1,33},{33,65},{65,97},{2,34},{34,66},{66,9... | collective-permute-start | bytes 24584 | tf_op jit(solution)/shard_map/ppermute | solution.py:28
  1206.3 58.8 %collective-permute-start.33 = (f32[1,4,1,512]{3,2,1,0:T(1,128)S(1)}, f32[1,4,1,512]{3,2,1,0:T(1,128)S(1)}, u32[]{:S(2)}, u32[]{:S(2)}) collective-permute-start(f32[1,4,1,512]{3,2,1,0:T(1,128)S(1)} %get-tuple-element.33), channel_id=1, source_target_pairs={{32,0},{64,32},{96,64},{33,1},{65,33},{97,65},{34,2},{66,34},{98,6... | collective-permute-start | bytes 24584 | tf_op jit(solution)/shard_map/ppermute | solution.py:30
  1265.2 4.8 collective-permute-start.34
  1267.9 6.2 collective-permute-start.35
  1276.6 76.2 %collective-permute-start.36 = (f32[1,1,64,512]{3,2,1,0:T(8,128)}, f32[1,1,64,512]{3,2,1,0:T(8,128)S(1)}, u32[]{:S(2)}, u32[]{:S(2)}) collective-permute-start(f32[1,1,64,512]{3,2,1,0:T(8,128)} %get-tuple-element.44), channel_id=1, source_target_pairs={{0,128},{128,256},{256,384},{1,129},{129,257},{257,385},{2,130},{1... | collective-permute-start | bytes 393224 | tf_op jit(solution)/shard_map/ppermute | solution.py:28
  1294.0 58.8 %collective-permute-start.37 = (f32[1,1,64,512]{3,2,1,0:T(8,128)}, f32[1,1,64,512]{3,2,1,0:T(8,128)S(1)}, u32[]{:S(2)}, u32[]{:S(2)}) collective-permute-start(f32[1,1,64,512]{3,2,1,0:T(8,128)} %get-tuple-element.45), channel_id=1, source_target_pairs={{128,0},{256,128},{384,256},{129,1},{257,129},{385,257},{130,2},{2... | collective-permute-start | bytes 393224 | tf_op jit(solution)/shard_map/ppermute | solution.py:30
  1352.9 8.9 collective-permute-start.38
  1358.1 6.5 collective-permute-start.39
  1364.7 5.7 collective-permute-start.40
  1368.3 5.9 collective-permute-start.41
where the time goes:
time: 1390 us; the launch traced here: 1380 us
  blocking collectives  994 us (72%)
  starting transfers between devices  294 us (21%)
  waiting for transfers between devices  51.1 us (4%)
  other arithmetic  13.9 us (1%)
  matrix products  13.9 us (1%)
    psum x8, blocking collectives, shards(): results[section] = lax.psum(placed, 'col')  453 us
    unnamed x6, blocking collectives  344 us
    ppermute x21, starting transfers between devices, padded(): lax.ppermute(tail, axis, [(i, (i + 1) % count) for i in range(ends)])  254 us
    psum x2, blocking collectives, shards(): rhs = lax.psum(local_rhs, ('layer', 'row', 'col')) * (restrict_scale / TILE)  198 us
    ppermute x21, waiting for transfers between devices, padded(): lax.ppermute(head, axis, [((i + 1) % count, i) for i in range(ends)])  45.7 us
    ppermute x21, starting transfers between devices, padded(): lax.ppermute(head, axis, [((i + 1) % count, i) for i in range(ends)])  39.5 us
  transfers between devices with their start and end apart: 42, of which 18 were waited for; matrix products, arithmetic and copies ran while one was open for 1% of the time, Pallas kernels for 0%

commit v1 on v0

v1 whole, which is shorter than its diff:
```python
import jax
import jax.numpy as jnp
from jax import lax
from jax.experimental import pallas as pl
from jax.experimental.pallas import tpu as pltpu
from jax.sharding import PartitionSpec as P

F32 = jnp.float32
BF16 = jnp.bfloat16
MESH = pl.DeviceIdType.MESH

TILE = 16
PANEL = 512
NPANEL = 4
NX, NY = 4, 8
NCOL = NX * NY
ROWS, COLS = 64, 512
SHARE = PANEL // NCOL
HALF = SHARE // 2

pad_gain = 8.0
bound_low = 0.1
bound_high = 1.9
restrict_scale = 0.25
prolong_scale = 0.5
theta = (bound_high + bound_low) / 2.0
delta = (bound_high - bound_low) / 2.0
sigma = theta / delta


def iota(shape, axis):
    return lax.broadcasted_iota(jnp.int32, shape, axis)


def pieces(x):
    high = x.astype(BF16).astype(F32)
    rest = x - high
    mid = rest.astype(BF16).astype(F32)
    return high, mid, rest - mid


def stacked(x):
    return jnp.concatenate(pieces(x), axis=0).astype(BF16)


def added(y):
    n = y.shape[0] // 3
    return y[:n] + y[n : 2 * n] + y[2 * n :]


def dot(a, b):
    return lax.dot_general(a, b, (((1,), (0,)), ((), ())), preferred_element_type=F32)


def dot_t(a, b):
    return lax.dot_general(a, b, (((1,), (1,)), ((), ())), preferred_element_type=F32)


def kernel(
    src, cond, via, vmap, pad, pt, piv, coup,
    drop_out, ports_out,
    S, V, INV, DP, VS, Q, T, CH, HSEND, HALO, RSEND, RIM, CSEND, SIDE,
    G, PART, ZSEND, Z, XM, X, CSND, CZ, CXM, CX, SBM, SB, LANES, ROWM, E4, MAPS, LIFT,
    hs, hr, gys, gyr, gxs, gxr, gfs, gfr, gbs, gbr, zs, zr, xs, xr, bs, br,
):
    l, r, c = lax.axis_index("layer"), lax.axis_index("row"), lax.axis_index("col")
    core = lax.rem(l, 2)
    x, y = c // NY, lax.rem(c, NY)

    def at_col(px, py):
        return (l, r, px * NY + py)

    group = [(lax.rem(l + d % 4, 4), lax.rem(r + d // 4, 4), c) for d in range(1, 16)]
    plane_peers = [(l, r, lax.rem(c + d, NCOL)) for d in range(1, NCOL)]
    sibling = (l + 1 - 2 * core, r, c)

    barrier = pltpu.get_barrier_semaphore()
    for peer in group + plane_peers:
        pl.semaphore_signal(barrier, inc=1, device_id=peer, device_id_type=MESH)

    def remote(a, b, ssem, rsem, peer):
        return pltpu.make_async_remote_copy(
            src_ref=a, dst_ref=b, send_sem=ssem, recv_sem=rsem, device_id=peer, device_id_type=MESH
        )

    for p in range(2):
        S[p] = jnp.sqrt(cond[p])
        V[p] = jnp.sqrt(via[p]) * vmap[p].astype(F32)
    E4[...] = jnp.where(
        iota((COLS, 128), 0) // TILE == lax.rem(iota((COLS, 128), 1), 32), 1.0, 0.0
    ).astype(BF16)

    def tile_row(plane):
        parts = [plane[TILE * a : TILE * a + 8] + plane[TILE * a + 8 : TILE * a + 16] for a in range(4)]
        sums = added(dot(stacked(jnp.concatenate(parts, axis=0)), E4[...]))
        own = iota((32, 128), 0) // 8 == iota((32, 128), 1) // 32
        return jnp.sum(jnp.where(own, sums, 0.0), axis=0, keepdims=True)

    zero_plane = jnp.zeros((ROWS, COLS), F32)

    @pl.when(l == 0)
    def _():
        for rd in range(6):
            HALO[rd, 0] = zero_plane

    @pl.when(l == 3)
    def _():
        for rd in range(6):
            HALO[rd, 1] = zero_plane

    @pl.when(r == 0)
    def _():
        for rd in range(6):
            RIM[rd, 0] = jnp.zeros((2, COLS), F32)

    @pl.when(r == 3)
    def _():
        for rd in range(6):
            RIM[rd, 1] = jnp.zeros((2, COLS), F32)

    @pl.when(c == 0)
    def _():
        for rd in range(6):
            SIDE[rd, 0] = jnp.zeros((1, 128), F32)

    @pl.when(c == NCOL - 1)
    def _():
        for rd in range(6):
            SIDE[rd, 1] = jnp.zeros((1, 128), F32)

    def layer_copies(rd):
        up = remote(HSEND.at[rd, 1], HALO.at[rd, 0], hs.at[rd, 0], hr.at[rd, 0], (lax.rem(l + 1, 4), r, c))
        down = remote(HSEND.at[rd, 0], HALO.at[rd, 1], hs.at[rd, 1], hr.at[rd, 1], (lax.rem(l + 3, 4), r, c))
        return ((l < 3, up, l > 0), (l > 0, down, l < 3))

    def rim_copies(rd):
        south = remote(RSEND.at[rd, 1], RIM.at[rd, 0], hs.at[rd, 2], hr.at[rd, 2], (l, lax.rem(r + 1, 4), c))
        north = remote(RSEND.at[rd, 0], RIM.at[rd, 1], hs.at[rd, 3], hr.at[rd, 3], (l, lax.rem(r + 3, 4), c))
        east = remote(CSEND.at[rd, 1], SIDE.at[rd, 0], hs.at[rd, 4], hr.at[rd, 4], (l, r, lax.rem(c + 1, NCOL)))
        west = remote(
            CSEND.at[rd, 0], SIDE.at[rd, 1], hs.at[rd, 5], hr.at[rd, 5], (l, r, lax.rem(c + NCOL - 1, NCOL))
        )
        return (
            (r < 3, south, r > 0),
            (r > 0, north, r < 3),
            (c < NCOL - 1, east, c > 0),
            (c > 0, west, c < NCOL - 1),
        )

    def start(copies):
        for sends, copy, _ in copies:
            @pl.when(sends)
            def _():
                copy.start()

    def arrive(copies):
        for _, copy, receives in copies:
            @pl.when(receives)
            def _():
                copy.wait_recv()

    def left(copies):
        for sends, copy, _ in copies:
            @pl.when(sends)
            def _():
                copy.wait_send()

    def send_layers(rd, h):
        for p in range(2):
            HSEND[rd, p] = h[p]
        start(layer_copies(rd))

    def send_rims(rd, g):
        for p in range(2):
            RSEND[rd, 0, p : p + 1] = g[p][:1]
            RSEND[rd, 1, p : p + 1] = g[p][ROWS - 1 :]
        first = jnp.concatenate([g[0][:, :128], g[1][:, :128]], axis=0)
        last = jnp.concatenate([g[0][:, COLS - 128 :], g[1][:, COLS - 128 :]], axis=0)
        CSEND[rd, 0] = first.T[:1]
        CSEND[rd, 1] = last.T[127:]
        start(rim_copies(rd))

    def column(rim):
        return jnp.broadcast_to(rim, (128, 128)).T

    row_at = iota((ROWS, COLS), 0)
    col_at = iota((ROWS, 128), 1)

    def from_east(g, side):
        moved = pltpu.roll(g, COLS - 1, 1)
        edge = jnp.where(col_at == 127, side, moved[:, COLS - 128 :])
        return jnp.concatenate([moved[:, : COLS - 128], edge], axis=1)

    def from_west(g, side):
        moved = pltpu.roll(g, 1, 1)
        edge = jnp.where(col_at == 0, side, moved[:, :128])
        return jnp.concatenate([edge, moved[:, 128:]], axis=1)

    def from_south(g, rim):
        return jnp.where(row_at == ROWS - 1, rim, pltpu.roll(g, ROWS - 1, 0))

    def from_north(g, rim):
        return jnp.where(row_at == 0, rim, pltpu.roll(g, 1, 0))

    def plane_sum(g, north, south, west, east):
        west, east = column(west), column(east)
        out = []
        for p in range(2):
            rows = slice(ROWS * p, ROWS * (p + 1))
            out.append(
                from_north(g[p], north[p : p + 1])
                + from_south(g[p], south[p : p + 1])
                + from_west(g[p], west[rows])
                + from_east(g[p], east[rows])
            )
        return out

    def received_sum(rd, g):
        return plane_sum(g, RIM[rd, 0], RIM[rd, 1], SIDE[rd, 0], SIDE[rd, 1])

    def group_copies(it, rows, buf, send):
        slot = r * 4 + l
        return [
            remote(send, buf.at[slot], zs.at[it, d], zr.at[it, d], peer) for d, peer in enumerate(group)
        ]

    def plane_copies(it, send, buf, ss, rs):
        return [remote(send, buf.at[c], ss.at[it, d], rs.at[it, d], peer) for d, peer in enumerate(plane_peers)]

    rim0 = [S[0], S[1]]
    plane = src[0] + src[1]
    ZSEND[0] = tile_row(plane)

    lane_of = []
    for k in range(NPANEL):
        tile = pt[k : k + 1, :]
        arow, acol = tile // 1024, lax.rem(tile, 1024)
        lane = lax.rem(arow, 4) * 32 + lax.rem(acol, 32)
        maprow = (acol // 32) * 4 + arow // 4
        LANES[k] = jnp.where(iota((128, PANEL), 0) == lane, 1.0, 0.0).astype(BF16)
        ROWM[k : k + 1] = maprow

    pl.semaphore_wait(barrier, 15 + 31)

    send_layers(0, [V[0], V[1]])
    send_rims(0, rim0)

    G[core, x, y] = coup[:, pl.ds(pl.multiple_of(core * HALF, HALF), HALF), :]
    mine = G.at[core, x, y]
    copies_y = [
        remote(mine, mine, gys.at[d - 1], gyr.at[d - 1], at_col(x, lax.rem(y + d, NY))) for d in range(1, NY)
    ]

    def copies_x(d):
        piece = G.at[core, x, lax.rem(y + NY - d, NY)]
        return [
            remote(piece, piece, gxs.at[s, d], gxr.at[s, d], at_col(lax.rem(x + step, NX), y))
            for s, step in enumerate((1, 3))
        ]

    turn = 1 - 2 * core

    def copy_forward(d):
        piece = G.at[core, lax.rem(x - turn + NX, NX), lax.rem(y + NY - d, NY)]
        return remote(piece, piece, gfs.at[d], gfr.at[d], at_col(lax.rem(x + turn + NX, NX), y))

    def copy_sibling(j):
        block = G.at[core, lax.rem(x + j, NX)]
        return remote(block, block, gbs.at[j], gbr.at[j], sibling)

    group_first = group_copies(0, 1, Z.at[0], ZSEND.at[0])
    for copy in group_first:
        copy.start()
    for d in (1, 7, 2, 6, 3, 5, 4):
        copies_y[d - 1].start()
    for copy in copies_x(0):
        copy.start()

    def forward_x(*ds):
        for d in ds:
            copies_y[d - 1].wait_recv()
            for copy in copies_x(d):
                copy.start()

    def forward_more(*ds):
        for d in ds:
            for copy in copies_x(d):
                copy.wait_recv()
            copy_forward(d).start()

    arrive(layer_copies(0))
    arrive(rim_copies(0))
    s = [S[0], S[1]]
    v = [V[0], V[1]]
    around = received_sum(0, s)
    top = (l == 3).astype(F32)
    pads = pad_gain * pad[...].astype(F32) * top
    vsum = [HALO[0, 0] + v[1], v[0] + HALO[0, 1]]
    for p in range(2):
        dp = s[p] * around[p]
        if p == 1:
            dp = dp + pads
        inv = 1.0 / (dp + v[p] * vsum[p])
        t = inv * src[p]
        DP[p], INV[p], VS[p], Q[p], T[p], CH[p] = dp, inv, vsum[p], t, t, t
    send_layers(1, [v[p] * T[p] for p in range(2)])
    send_rims(1, [s[p] * T[p] for p in range(2)])

    forward_x(1, 7)

    def gather_plane(it, buf, msg, bufx):
        for q in range(4):
            total = buf[4 * q]
            for k in range(1, 4):
                total = total + buf[4 * q + k]
            msg[q : q + 1] = total
        bufx[c] = msg[...]
        out = plane_copies(it, msg, bufx, xs, xr)
        for copy in out:
            copy.start()
        return out

    Z[0, r * 4 + l] = ZSEND[0]
    for copy in group_first:
        copy.wait_recv()
    plane_first = gather_plane(0, Z.at[0], XM.at[0], X.at[0])

    west_col, east_col = SIDE[0, 0], SIDE[0, 1]
    east_side = column(east_col)
    edge_e = jnp.zeros((ROWS, COLS), F32)
    edge_s = jnp.zeros((ROWS, COLS), F32)
    for p in range(2):
        edge_e = edge_e + s[p] * from_east(s[p], east_side[ROWS * p : ROWS * (p + 1)])
        edge_s = edge_s + s[p] * from_south(s[p], RIM[0, 1, p : p + 1])
    edge_e = jnp.where(lax.rem(iota((ROWS, COLS), 1), TILE) == TILE - 1, edge_e, 0.0)
    edge_s = jnp.where(lax.rem(iota((ROWS, COLS), 0), TILE) == TILE - 1, edge_s, 0.0)
    for k, field in enumerate((pads, edge_e, edge_s)):
        CSND[k : k + 1] = tile_row(field)
    CZ[r * 4 + l] = CSND[...]
    group_coef = group_copies(1, 3, CZ, CSND)
    for copy in group_coef:
        copy.start()

    forward_x(2, 6)

    def sweep(rd, rho, s, v):
        rho_new = 1.0 / (2.0 * sigma - rho)
        t = [T[0], T[1]]
        arrive(rim_copies(rd))
        around = received_sum(rd, [s[p] * t[p] for p in range(2)])
        arrive(layer_copies(rd))
        vert = [HALO[rd, 0] + v[1] * t[1], v[0] * t[0] + HALO[rd, 1]]
        for p in range(2):
            remain = Q[p] - t[p] + INV[p] * (s[p] * around[p] + v[p] * vert[p])
            ch = (rho_new * rho) * CH[p] + (2.0 * rho_new / delta) * remain
            CH[p] = ch
            T[p] = t[p] + ch
        return rho_new

    rho = sweep(1, 1.0 / sigma, s, v)
    send_layers(2, [v[p] * T[p] for p in range(2)])
    send_rims(2, [s[p] * T[p] for p in range(2)])

    forward_x(3, 5, 4)
    copy_sibling(0).start()

    for copy in group_coef:
        copy.wait_recv()
    for q in range(4):
        total = CZ[4 * q]
        for k in range(1, 4):
            total = total + CZ[4 * q + k]
        for k in range(3):
            CXM[k, q : q + 1] = total[k : k + 1]
    CX[c] = CXM[...]
    plane_coef = plane_copies(1, CXM, CX, xs, xr)
    for copy in plane_coef:
        copy.start()

    sweep(2, rho, s, v)
    send_layers(3, [v[p] * T[p] for p in range(2)])
    send_rims(3, [s[p] * T[p] for p in range(2)])

    forward_more(0, 1, 7)

    def tile_map(load):
        return jnp.concatenate([load(k) for k in range(NCOL)], axis=0)

    def row_mask(k):
        return iota((128, PANEL), 0) == ROWM[k : k + 1]

    def select_ports(tiles):
        parts = stacked(tiles)
        out = []
        for k in range(NPANEL):
            picked = added(dot(parts, LANES[k]))
            out.append(
                jnp.sum(jnp.where(row_mask(k), picked, 0.0), axis=0, keepdims=True) * (restrict_scale / TILE)
            )
        return out

    for copy in plane_first:
        copy.wait_recv()
    rhs = select_ports(tile_map(lambda k: X[0, k]))

    arrive(rim_copies(3))
    arrive(layer_copies(3))
    around = received_sum(3, [s[p] * T[p] for p in range(2)])
    vert = [HALO[3, 0] + v[1] * T[1], v[0] * T[0] + HALO[3, 1]]
    for p in range(2):
        t = T[p]
        Q[p] = src[p] - ((DP[p] + v[p] * VS[p]) * t - s[p] * around[p] - v[p] * vert[p])
    ZSEND[1] = tile_row(Q[0] + Q[1])
    Z[1, r * 4 + l] = ZSEND[1]
    group_second = group_copies(2, 1, Z.at[1], ZSEND.at[1])
    for copy in group_second:
        copy.start()

    forward_more(2, 6, 3, 5, 4)
    copy_sibling(1).start()
    copy_sibling(3).start()
    for copy in group_second:
        copy.wait_recv()
    plane_second = gather_plane(2, Z.at[1], XM.at[1], X.at[1])
    for d in range(NY):
        copy_forward(d).wait_recv()
    copy_sibling(2).start()
    for j in range(NX):
        copy_sibling(j).wait_recv()

    def minus(k, f):
        wide = jnp.broadcast_to(f, (8, PANEL))

        def body(i, carry):
            px, py = i // NY, lax.rem(i, NY)
            for h in range(2):
                prod = G[h, px, py, k] * wide
                part = prod[:, :128] + prod[:, 128:256] + prod[:, 256:384] + prod[:, 384:]
                PART[pl.ds(pl.multiple_of(i * SHARE + h * HALF, HALF), HALF)] = part
            return carry

        lax.fori_loop(0, NCOL, body, 0, unroll=8)
        return jnp.concatenate(
            [jnp.sum(PART[128 * j : 128 * (j + 1)].T, axis=0, keepdims=True) for j in range(4)], axis=1
        )

    def minus_transposed(k, f):
        for j in range(4):
            PART[128 * j : 128 * (j + 1)] = column(f[:, 128 * j : 128 * (j + 1)])

        def body(i, acc):
            px, py = i // NY, lax.rem(i, NY)
            for h in range(2):
                w = PART[pl.ds(pl.multiple_of(i * SHARE + h * HALF, HALF), HALF)]
                acc = acc + G[h, px, py, k] * jnp.concatenate([w] * 4, axis=1)
            return acc

        acc = lax.fori_loop(0, NCOL, body, jnp.zeros((8, PANEL), F32), unroll=8)
        return jnp.sum(acc, axis=0, keepdims=True)

    def solve_first(it, rhs):
        forward = [rhs[0]]
        for k in range(1, NPANEL):
            forward.append(rhs[k] - minus(k - 1, forward[-1]))
        rows = []
        for k in range(NPANEL):
            prod = piv[k] * forward[k]
            rows.append(prod[:, :128] + prod[:, 128:256] + prod[:, 256:384] + prod[:, 384:])
        rows.append(jnp.zeros((128 - NPANEL * SHARE, 128), F32))
        SBM[it] = jnp.sum(jnp.concatenate(rows, axis=0).T, axis=0, keepdims=True)
        SB[it, c] = SBM[it]
        copies = plane_copies(it, SBM.at[it], SB.at[it], bs, br)
        for copy in copies:
            copy.start()
        return copies

    def solve_second(it, copies):
        for copy in copies:
            copy.wait_recv()
        got = stacked(jnp.concatenate([SB[it, k] for k in range(NCOL)], axis=0))
        owner = iota((NCOL, PANEL), 1) // SHARE == iota((NCOL, PANEL), 0)
        scaled = []
        for k in range(NPANEL):
            spread = jnp.where(
                iota((128, PANEL), 0) == k * SHARE + lax.rem(iota((128, PANEL), 1), SHARE), 1.0, 0.0
            ).astype(BF16)
            value = added(dot(got, spread))
            scaled.append(jnp.sum(jnp.where(owner, value, 0.0), axis=0, keepdims=True))
        ports = [None] * NPANEL
        ports[NPANEL - 1] = scaled[NPANEL - 1]
        for k in range(NPANEL - 2, -1, -1):
            ports[k] = scaled[k] - minus_transposed(k, ports[k + 1])
        return ports

    def lifted_rows(ports, wanted):
        total = jnp.zeros((24, 128), F32)
        for k in range(NPANEL):
            parts = pieces(ports[k] * prolong_scale)
            masks = [ROWM[k : k + 1] == w for w in wanted]
            masks += [masks[0]] * (8 - len(masks))
            rows = [jnp.where(m, part, 0.0) for part in parts for m in masks]
            total = total + dot_t(jnp.concatenate(rows, axis=0).astype(BF16), LANES[k])
        return added(total)

    lane_row = iota((1, 128), 1)

    def spread_rows(rows):
        return added(dot_t(stacked(rows), E4[...]))

    def field_of(own):
        return jnp.concatenate([jnp.where(lane_row // 32 == min(a, 3), own, 0.0) for a in range(4)], axis=0)

    first = solve_first(0, rhs)
    ports1 = solve_second(0, first)

    own_row = c * 4 + r
    none = jnp.int32(-1)
    wanted = [
        own_row,
        jnp.where(r > 0, own_row - 1, none),
        jnp.where(r < 3, own_row + 1, none),
        jnp.where(c > 0, own_row - 4, none),
        jnp.where(c < NCOL - 1, own_row + 4, none),
    ]
    near = lifted_rows(ports1, wanted)
    level = jnp.concatenate(
        [
            field_of(near[0:1]),
            jnp.where(lane_row // 32 == 3, near[1:2], 0.0),
            jnp.where(lane_row // 32 == 0, near[2:3], 0.0),
            jnp.zeros((2, 128), F32),
        ],
        axis=0,
    )
    level = spread_rows(level)
    lift = jnp.concatenate(
        [jnp.broadcast_to(level[a : a + 1], (TILE, COLS)) for a in range(4)], axis=0
    )
    LIFT[...] = lift
    at_row = lax.rem(iota((128, 128), 1), ROWS) // TILE * 32
    pick_w = jnp.where(iota((128, 128), 0) == at_row + 31, 1.0, 0.0).astype(BF16)
    pick_e = jnp.where(iota((128, 128), 0) == at_row, 1.0, 0.0).astype(BF16)
    side_w = added(dot(stacked(near), pick_w))[3:4]
    side_e = added(dot(stacked(near), pick_e))[4:5]
    lifted_around = plane_sum(
        [s[p] * lift for p in range(2)],
        RIM[0, 0] * level[4:5],
        RIM[0, 1] * level[5:6],
        SIDE[0, 0] * side_w,
        SIDE[0, 1] * side_e,
    )
    for p in range(2):
        t3 = T[p]
        resid = Q[p] - (DP[p] * lift - s[p] * lifted_around[p])
        t = INV[p] * resid
        drop_out[p] = lift + t3
        Q[p], T[p], CH[p] = t, t, t
    send_layers(4, [v[p] * T[p] for p in range(2)])
    send_rims(4, [s[p] * T[p] for p in range(2)])

    lifted_map = jnp.zeros((384, 128), F32)
    for k in range(NPANEL):
        mask = row_mask(k)
        parts = [jnp.where(mask, part, 0.0).astype(BF16) for part in pieces(ports1[k] * prolong_scale)]
        lifted_map = lifted_map + dot_t(jnp.concatenate(parts, axis=0), LANES[k])
    lifted_map = added(lifted_map)
    for copy in plane_coef:
        copy.wait_recv()
    pads_map = tile_map(lambda k: CX[k, 0])
    edge_e = tile_map(lambda k: CX[k, 1])
    edge_s = tile_map(lambda k: CX[k, 2])
    lanes = iota((128, 128), 1)

    def tile_east(a):
        ahead = pltpu.roll(a, 124, 0)
        return jnp.where(lax.rem(lanes, 32) == 31, pltpu.roll(ahead, 31, 1), pltpu.roll(a, 127, 1))

    def tile_west(a):
        behind = pltpu.roll(a, 4, 0)
        return jnp.where(lax.rem(lanes, 32) == 0, pltpu.roll(behind, 97, 1), pltpu.roll(a, 1, 1))

    def tile_south(a):
        below = pltpu.roll(a, 127, 0)
        return jnp.where(lanes // 32 == 3, pltpu.roll(below, 96, 1), pltpu.roll(a, 96, 1))

    def tile_north(a):
        above = pltpu.roll(a, 1, 0)
        return jnp.where(lanes // 32 == 0, pltpu.roll(above, 32, 1), pltpu.roll(a, 32, 1))

    flow_e = edge_e * (lifted_map - tile_east(lifted_map))
    flow_s = edge_s * (lifted_map - tile_south(lifted_map))
    coarse = pads_map * lifted_map + flow_e - tile_west(flow_e) + flow_s - tile_north(flow_s)

    for copy in plane_second:
        copy.wait_recv()
    rhs = select_ports(tile_map(lambda k: X[1, k]) - coarse)
    second = solve_first(1, rhs)

    rho = sweep(4, 1.0 / sigma, s, v)
    send_layers(5, [v[p] * T[p] for p in range(2)])
    send_rims(5, [s[p] * T[p] for p in range(2)])

    ports2 = solve_second(1, second)
    for k in range(NPANEL):
        ports_out[k : k + 1] = ports2[k]
    near = lifted_rows(ports2, [own_row])
    level = spread_rows(jnp.concatenate([field_of(near[0:1])] * 2, axis=0))
    sweep(5, rho, s, v)
    for p in range(2):
        for a in range(4):
            rows = slice(TILE * a, TILE * (a + 1))
            drop_out[p, rows] = drop_out[p, rows] + T[p, rows] + level[a : a + 1]

    for rd in range(6):
        left(layer_copies(rd))
        left(rim_copies(rd))
    for copy in copies_y + group_first + group_coef + group_second:
        copy.wait_send()
    for copy in plane_first + plane_coef + plane_second + first + second:
        copy.wait_send()
    for d in range(NY):
        for copy in copies_x(d):
            copy.wait_send()
        copy_forward(d).wait_send()
    for j in range(NX):
        copy_sibling(j).wait_send()


def shards(*args):
    vmem = pl.BlockSpec(memory_space=pltpu.VMEM)
    field = pltpu.VMEM((2, ROWS, COLS), F32)
    dma = pltpu.SemaphoreType.DMA
    return pl.pallas_call(
        kernel,
        out_shape=(
            jax.ShapeDtypeStruct((2, ROWS, COLS), F32),
            jax.ShapeDtypeStruct((NPANEL, PANEL), F32),
        ),
        in_specs=[vmem] * 8,
        out_specs=(vmem, vmem),
        scratch_shapes=[
            field, field, field, field, field, field, field, field,
            pltpu.VMEM((6, 2, ROWS, COLS), F32),
            pltpu.VMEM((6, 2, ROWS, COLS), F32),
            pltpu.VMEM((6, 2, 2, COLS), F32),
            pltpu.VMEM((6, 2, 2, COLS), F32),
            pltpu.VMEM((6, 2, 1, 128), F32),
            pltpu.VMEM((6, 2, 1, 128), F32),
            pltpu.VMEM((2, NX, NY, NPANEL - 1, HALF, PANEL), F32),
            pltpu.VMEM((PANEL, 128), F32),
            pltpu.VMEM((2, 1, 128), F32),
            pltpu.VMEM((2, 16, 1, 128), F32),
            pltpu.VMEM((2, 4, 128), F32),
            pltpu.VMEM((2, NCOL, 4, 128), F32),
            pltpu.VMEM((3, 128), F32),
            pltpu.VMEM((16, 3, 128), F32),
            pltpu.VMEM((3, 4, 128), F32),
            pltpu.VMEM((NCOL, 3, 4, 128), F32),
            pltpu.VMEM((2, 1, 128), F32),
            pltpu.VMEM((2, NCOL, 1, 128), F32),
            pltpu.VMEM((NPANEL, 128, PANEL), BF16),
            pltpu.VMEM((NPANEL, PANEL), jnp.int32),
            pltpu.VMEM((COLS, 128), BF16),
            pltpu.VMEM((8, 128), F32),
            pltpu.VMEM((ROWS, COLS), F32),
            dma((6, 6)), dma((6, 6)),
            dma((7,)), dma((7,)),
            dma((2, 8)), dma((2, 8)),
            dma((8,)), dma((8,)),
            dma((4,)), dma((4,)),
            dma((3, 15)), dma((3, 15)),
            dma((3, 31)), dma((3, 31)),
            dma((2, 31)), dma((2, 31)),
        ],
        compiler_params=pltpu.CompilerParams(
            collective_id=0, has_side_effects=True, vmem_limit_bytes=48 * 1024 * 1024
        ),
        cost_estimate=pl.CostEstimate(flops=100_000_000, bytes_accessed=2_000_000, transcendentals=300_000),
        name="grid",
    )(*args)


def solution(mesh):
    placed = (
        P("layer", "row", "col"),
        P("layer", "row", "col"),
        P("layer", "row", "col"),
        P("layer", "row", "col"),
        P("row", "col"),
        P(),
        P(None, "col", None),
        P(None, "col", None),
    )
    return jax.shard_map(
        shards,
        mesh=mesh,
        in_specs=placed,
        out_specs=(P("layer", "row", "col"), P()),
        check_vma=False,
    )
```

time: 1390 us -> 78.9 us (0.06)
  blocking collectives: 994 us -> 0 us
  starting transfers between devices: 294 us -> 0 us
  Pallas kernels: 0 us -> 69.4 us
  waiting for transfers between devices: 51.1 us -> 0 us
  matrix products: 13.9 us -> 0 us
  other arithmetic: 13.9 us -> 0 us
    psum x10 -> x0, blocking collectives: 650 us -> none  [the longest x8 453 us: shards(): results[section] = lax.psum(placed, 'col')]
    unnamed x6 -> x0, blocking collectives: 344 us -> none
    ppermute x42 -> x0, starting transfers between devices: 294 us -> none  [the longest x21 254 us: padded(): lax.ppermute(tail, axis, [(i, (i + 1) % count) for i in range(ends)])]
    pallas_call x0 -> x1, Pallas kernels: none -> 69.4 us  [shards(): pl.pallas_call(kernel, out_shape=(jax.ShapeDtypeStruct((2, ROWS, COLS), F...]
    ppermute x42 -> x0, waiting for transfers between devices: 51.1 us -> none  [the longest x21 45.7 us: padded(): lax.ppermute(head, axis, [((i + 1) % count, i) for i in range(ends)])]
  transfers between devices with their start and end apart: 42 -> 0, of which waited for: 18 -> 0; matrix products, arithmetic and copies ran while one was open for 1% -> 0% of each run, Pallas kernels for 0% -> 0%
where the time goes in v1:
time: 78.9 us; the launch traced here: 78.6 us
  Pallas kernels  69.4 us (88%)
  local copies, waits for them, and re-layouts  8.49 us (11%)
    pallas_call x1, Pallas kernels, shards(): pl.pallas_call(kernel, out_shape=(jax.ShapeDtypeStruct((2, ROWS, COLS), F...  69.4 us
    unnamed x18, local copies, waits for them, and re-layouts  8.49 us

profile of v1, /device:TPU:1, one launch (start us, length us, event | category | flops | bytes accessed | tf_op | source)
XLA Modules:
  0.0 78.6 jit_solution(5467705074462295831)
XLA Ops:
  0.6 0.0 copy-start
  0.6 0.9 %copy-done = f32[2,64,512]{2,1,0:T(8,128)S(1)} copy-done((f32[2,64,512]{2,1,0:T(8,128)S(1)}, f32[2,64,512]{2,1,0:T(8,128)}, u32[]{:S(2)}) %copy-start) | copy-done | bytes 262168
  1.6 0.0 copy-start.1
  1.6 0.9 %copy-done.1 = f32[2,64,512]{2,1,0:T(8,128)S(1)} copy-done((f32[2,64,512]{2,1,0:T(8,128)S(1)}, f32[2,64,512]{2,1,0:T(8,128)}, u32[]{:S(2)}) %copy-start.1) | copy-done | bytes 262168
  2.5 0.0 copy-start.2
  2.5 0.9 %copy-done.2 = f32[2,64,512]{2,1,0:T(8,128)S(1)} copy-done((f32[2,64,512]{2,1,0:T(8,128)S(1)}, f32[2,64,512]{2,1,0:T(8,128)}, u32[]{:S(2)}) %copy-start.2) | copy-done | bytes 262168
  3.5 0.0 copy-start.3
  3.5 0.9 %copy-done.3 = s32[2,64,512]{2,1,0:T(8,128)S(1)} copy-done((s32[2,64,512]{2,1,0:T(8,128)S(1)}, s32[2,64,512]{2,1,0:T(8,128)}, u32[]{:S(2)}) %copy-start.3) | copy-done | bytes 262168
  4.4 0.0 copy-start.4
  4.4 0.9 %copy-done.4 = s32[64,512]{1,0:T(8,128)S(1)} copy-done((s32[64,512]{1,0:T(8,128)S(1)}, s32[64,512]{1,0:T(8,128)}, u32[]{:S(2)}) %copy-start.4) | copy-done | bytes 131096
  5.3 0.0 copy-start.5
  5.3 0.9 %copy-done.5 = f32[4,16,512]{2,1,0:T(8,128)S(1)} copy-done((f32[4,16,512]{2,1,0:T(8,128)S(1)}, f32[4,16,512]{2,1,0:T(8,128)}, u32[]{:S(2)}) %copy-start.5) | copy-done | bytes 131096
  6.2 0.0 copy-start.6
  6.2 0.9 %copy-done.6 = f32[3,16,512]{2,1,0:T(8,128)S(1)} copy-done((f32[3,16,512]{2,1,0:T(8,128)S(1)}, f32[3,16,512]{2,1,0:T(8,128)}, u32[]{:S(2)}) %copy-start.6) | copy-done | bytes 98328
  7.1 0.0 copy-start.7
  7.1 0.7 copy-done.7
  7.8 69.4 %grid.1 = (f32[2,64,512]{2,1,0:T(8,128)S(1)}, f32[4,512]{1,0:T(4,128)S(1)}) custom-call(f32[2,64,512]{2,1,0:T(8,128)S(1)} %copy-done, f32[2,64,512]{2,1,0:T(8,128)S(1)} %copy-done.1, f32[2,64,512]{2,1,0:T(8,128)S(1)} %copy-done.2, s32[2,64,512]{2,1,0:T(8,128)S(1)} %copy-done.3, s32[64,512]{1,0:T(8,128)S(1)} %copy-done.4, s32[4,512]{1,0:T(4,128)S(1)} %copy-done.7, ...), custom_call_target="tpu_custom_call" | custom-call | flops 100000000 | bytes 2000000 | tf_op jit(solution)/shard_map/grid/pallas_call | solution.py:633
  77.3 0.7 copy.12
  78.0 0.6 copy.13
Async XLA Ops:
  0.6 1.0 %copy-start = (f32[2,64,512]{2,1,0:T(8,128)S(1)}, f32[2,64,512]{2,1,0:T(8,128)}, u32[]{:S(2)}) copy-start(f32[2,64,512]{2,1,0:T(8,128)} %src.1) | copy-start | bytes 786436
  1.6 0.9 %copy-start.1 = (f32[2,64,512]{2,1,0:T(8,128)S(1)}, f32[2,64,512]{2,1,0:T(8,128)}, u32[]{:S(2)}) copy-start(f32[2,64,512]{2,1,0:T(8,128)} %cond.1) | copy-start | bytes 786436
  2.5 0.9 %copy-start.2 = (f32[2,64,512]{2,1,0:T(8,128)S(1)}, f32[2,64,512]{2,1,0:T(8,128)}, u32[]{:S(2)}) copy-start(f32[2,64,512]{2,1,0:T(8,128)} %via.1) | copy-start | bytes 786436
  3.5 0.9 %copy-start.3 = (s32[2,64,512]{2,1,0:T(8,128)S(1)}, s32[2,64,512]{2,1,0:T(8,128)}, u32[]{:S(2)}) copy-start(s32[2,64,512]{2,1,0:T(8,128)} %vmap.1) | copy-start | bytes 786436
  4.4 0.9 %copy-start.4 = (s32[64,512]{1,0:T(8,128)S(1)}, s32[64,512]{1,0:T(8,128)}, u32[]{:S(2)}) copy-start(s32[64,512]{1,0:T(8,128)} %pad.1) | copy-start | bytes 393220
  5.3 0.9 %copy-start.5 = (f32[4,16,512]{2,1,0:T(8,128)S(1)}, f32[4,16,512]{2,1,0:T(8,128)}, u32[]{:S(2)}) copy-start(f32[4,16,512]{2,1,0:T(8,128)} %piv.1) | copy-start | bytes 393220
  6.2 0.9 %copy-start.6 = (f32[3,16,512]{2,1,0:T(8,128)S(1)}, f32[3,16,512]{2,1,0:T(8,128)}, u32[]{:S(2)}) copy-start(f32[3,16,512]{2,1,0:T(8,128)} %coup.1) | copy-start | bytes 294916
  7.1 0.7 copy-start.7

commit v2 on v1

--- a/solution.py
+++ b/solution.py
@@ -57,11 +57,13 @@
 
 
 def kernel(
-    src, cond, via, vmap, pad, pt, piv, coup,
+    src_in, cond_in, via_in, vmap_in, pad_in, pt_in, piv_in, coup_in,
     drop_out, ports_out,
+    src, cond, via, vmap, pad, pt, piv,
     S, V, INV, DP, VS, Q, T, CH, HSEND, HALO, RSEND, RIM, CSEND, SIDE,
-    G, PART, ZSEND, Z, XM, X, CSND, CZ, CXM, CX, SBM, SB, LANES, ROWM, E4, MAPS, LIFT,
-    hs, hr, gys, gyr, gxs, gxr, gfs, gfr, gbs, gbr, zs, zr, xs, xr, bs, br,
+    G, GP, FW, SL, PART, ZSEND, Z, XM, X, CSND, CZ, CXM, CX, SBM, SB, LANES, ROWM, E4, MAPS, LIFT,
+    ins, hs, hr, gys, gyr, gxs, gxr, gfs, gfr,
+    pys, pyr, pxs, pxr, pfs, pfr, ls, lr, gbs, gbr, zs, zr, xs, xr, bs, br,
 ):
     l, r, c = lax.axis_index("layer"), lax.axis_index("row"), lax.axis_index("col")
     core = lax.rem(l, 2)
@@ -83,9 +85,25 @@
             src_ref=a, dst_ref=b, send_sem=ssem, recv_sem=rsem, device_id=peer, device_id_type=MESH
         )
 
-    for p in range(2):
-        S[p] = jnp.sqrt(cond[p])
-        V[p] = jnp.sqrt(via[p]) * vmap[p].astype(F32)
+    inputs = [
+        pltpu.make_async_copy(a, b, ins.at[n])
+        for n, (a, b) in enumerate(
+            (
+                (via_in, via),
+                (vmap_in, vmap),
+                (cond_in, cond),
+                (coup_in.at[:, pl.ds(pl.multiple_of(core * HALF, HALF), HALF), :], G.at[core, x, y]),
+                (src_in, src),
+                (pt_in, pt),
+                (pad_in, pad),
+                (piv_in, piv),
+                (piv_in.at[l], GP.at[x, y]),
+            )
+        )
+    ]
+    for copy in inputs:
+        copy.start()
+
     E4[...] = jnp.where(
         iota((COLS, 128), 0) // TILE == lax.rem(iota((COLS, 128), 1), 32), 1.0, 0.0
     ).astype(BF16)
@@ -227,66 +245,103 @@
     def plane_copies(it, send, buf, ss, rs):
         return [remote(send, buf.at[c], ss.at[it, d], rs.at[it, d], peer) for d, peer in enumerate(plane_peers)]
 
-    rim0 = [S[0], S[1]]
-    plane = src[0] + src[1]
-    ZSEND[0] = tile_row(plane)
-
-    lane_of = []
+    for copy in inputs[:3]:
+        copy.wait()
+    for p in range(2):
+        S[p] = jnp.sqrt(cond[p])
+        V[p] = jnp.sqrt(via[p]) * vmap[p].astype(F32)
+    for copy in inputs[3:5]:
+        copy.wait()
+
+    pl.semaphore_wait(barrier, 15 + 31)
+
+    send_layers(0, [V[0], V[1]])
+    send_rims(0, [S[0], S[1]])
+
+    turn = 1 - 2 * core
+
+    class Ring:
+        def __init__(self, slot, ys, yr, xs, xr, fs, fr):
+            self.slot, self.xs, self.xr, self.fs, self.fr = slot, xs, xr, fs, fr
+            self.along_y = {}
+            for d, began, step in (
+                (1, 0, 1), (7, 0, NY - 1), (2, 0, 2), (6, 0, NY - 2),
+                (3, 1, 2), (5, NY - 1, NY - 2), (4, 2 * turn + NY, 2 * turn + NY),
+            ):
+                piece = slot(x, lax.rem(y + 2 * NY - began, NY))
+                self.along_y[d] = remote(
+                    piece, piece, ys.at[d - 1], yr.at[d - 1], at_col(x, lax.rem(y + step, NY))
+                )
+
+        def along_x(self, d):
+            piece = self.slot(x, lax.rem(y + NY - d, NY))
+            return [
+                remote(piece, piece, self.xs.at[s, d], self.xr.at[s, d], at_col(lax.rem(x + step, NX), y))
+                for s, step in enumerate((1, 3))
+            ]
+
+        def onward(self, d):
+            piece = self.slot(lax.rem(x - turn + NX, NX), lax.rem(y + NY - d, NY))
+            return remote(piece, piece, self.fs.at[d], self.fr.at[d], at_col(lax.rem(x + turn + NX, NX), y))
+
+        def begin(self):
+            for d in (1, 7, 2, 6):
+                self.along_y[d].start()
+
+        def pass_y(self, *ds):
+            for d in ds:
+                self.along_y[d].wait_recv()
+            for d in ds:
+                if d in (1, 7):
+                    self.along_y[{1: 3, 7: 5}[d]].start()
+            if 2 in ds:
+                self.along_y[4].start()
+
+        def send_x(self, *ds):
+            for d in ds:
+                for copy in self.along_x(d):
+                    copy.start()
+
+        def pass_x(self, *ds):
+            for d in ds:
+                for copy in self.along_x(d):
+                    copy.wait_recv()
+                self.onward(d).start()
+
+        def end(self):
+            for d in range(NY):
+                self.onward(d).wait_recv()
+
+        def sent(self):
+            for d in range(1, NY):
+                self.along_y[d].wait_send()
+            for d in range(NY):
+                for copy in self.along_x(d):
+                    copy.wait_send()
+                self.onward(d).wait_send()
+
+    lower = Ring(lambda px, py: G.at[core, px, py], gys, gyr, gxs, gxr, gfs, gfr)
+    panel = Ring(lambda px, py: GP.at[px, py], pys, pyr, pxs, pxr, pfs, pfr)
+
+    def copy_sibling(j):
+        block = G.at[core, lax.rem(x + j, NX)]
+        return remote(block, block, gbs.at[j], gbr.at[j], sibling)
+
+    lower.begin()
+    lower.send_x(0)
+    ZSEND[0] = tile_row(src[0] + src[1])
+    group_first = group_copies(0, 1, Z.at[0], ZSEND.at[0])
+    for copy in group_first:
+        copy.start()
+
+    for copy in inputs[5:]:
+        copy.wait()
     for k in range(NPANEL):
         tile = pt[k : k + 1, :]
         arow, acol = tile // 1024, lax.rem(tile, 1024)
         lane = lax.rem(arow, 4) * 32 + lax.rem(acol, 32)
-        maprow = (acol // 32) * 4 + arow // 4
         LANES[k] = jnp.where(iota((128, PANEL), 0) == lane, 1.0, 0.0).astype(BF16)
-        ROWM[k : k + 1] = maprow
-
-    pl.semaphore_wait(barrier, 15 + 31)
-
-    send_layers(0, [V[0], V[1]])
-    send_rims(0, rim0)
-
-    G[core, x, y] = coup[:, pl.ds(pl.multiple_of(core * HALF, HALF), HALF), :]
-    mine = G.at[core, x, y]
-    copies_y = [
-        remote(mine, mine, gys.at[d - 1], gyr.at[d - 1], at_col(x, lax.rem(y + d, NY))) for d in range(1, NY)
-    ]
-
-    def copies_x(d):
-        piece = G.at[core, x, lax.rem(y + NY - d, NY)]
-        return [
-            remote(piece, piece, gxs.at[s, d], gxr.at[s, d], at_col(lax.rem(x + step, NX), y))
-            for s, step in enumerate((1, 3))
-        ]
-
-    turn = 1 - 2 * core
-
-    def copy_forward(d):
-        piece = G.at[core, lax.rem(x - turn + NX, NX), lax.rem(y + NY - d, NY)]
-        return remote(piece, piece, gfs.at[d], gfr.at[d], at_col(lax.rem(x + turn + NX, NX), y))
-
-    def copy_sibling(j):
-        block = G.at[core, lax.rem(x + j, NX)]
-        return remote(block, block, gbs.at[j], gbr.at[j], sibling)
-
-    group_first = group_copies(0, 1, Z.at[0], ZSEND.at[0])
-    for copy in group_first:
-        copy.start()
-    for d in (1, 7, 2, 6, 3, 5, 4):
-        copies_y[d - 1].start()
-    for copy in copies_x(0):
-        copy.start()
-
-    def forward_x(*ds):
-        for d in ds:
-            copies_y[d - 1].wait_recv()
-            for copy in copies_x(d):
-                copy.start()
-
-    def forward_more(*ds):
-        for d in ds:
-            for copy in copies_x(d):
-                copy.wait_recv()
-            copy_forward(d).start()
+        ROWM[k : k + 1] = (acol // 32) * 4 + arow // 4
 
     arrive(layer_copies(0))
     arrive(rim_copies(0))
@@ -306,7 +361,8 @@
     send_layers(1, [v[p] * T[p] for p in range(2)])
     send_rims(1, [s[p] * T[p] for p in range(2)])
 
-    forward_x(1, 7)
+    lower.pass_y(1, 7)
+    lower.send_x(1, 7)
 
     def gather_plane(it, buf, msg, bufx):
         for q in range(4):
@@ -341,7 +397,8 @@
     for copy in group_coef:
         copy.start()
 
-    forward_x(2, 6)
+    lower.pass_y(2, 6)
+    lower.send_x(2, 6)
 
     def sweep(rd, rho, s, v):
         rho_new = 1.0 / (2.0 * sigma - rho)
@@ -361,7 +418,9 @@
     send_layers(2, [v[p] * T[p] for p in range(2)])
     send_rims(2, [s[p] * T[p] for p in range(2)])
 
-    forward_x(3, 5, 4)
+    lower.pass_y(3, 5, 4)
+    lower.send_x(3, 5, 4)
+    panel.begin()
     copy_sibling(0).start()
 
     for copy in group_coef:
@@ -381,7 +440,8 @@
     send_layers(3, [v[p] * T[p] for p in range(2)])
     send_rims(3, [s[p] * T[p] for p in range(2)])
 
-    forward_more(0, 1, 7)
+    lower.pass_x(0, 1, 7)
+    panel.pass_y(1, 7)
 
     def tile_map(load):
         return jnp.concatenate([load(k) for k in range(NCOL)], axis=0)
@@ -416,25 +476,28 @@
     for copy in group_second:
         copy.start()
 
-    forward_more(2, 6, 3, 5, 4)
+    lower.pass_x(2, 6, 3, 5, 4)
+    panel.pass_y(2, 6)
     copy_sibling(1).start()
     copy_sibling(3).start()
     for copy in group_second:
         copy.wait_recv()
     plane_second = gather_plane(2, Z.at[1], XM.at[1], X.at[1])
-    for d in range(NY):
-        copy_forward(d).wait_recv()
+    lower.end()
     copy_sibling(2).start()
+    panel.send_x(0, 1, 7, 2, 6)
+    panel.pass_y(3, 5, 4)
+    panel.send_x(3, 5, 4)
     for j in range(NX):
         copy_sibling(j).wait_recv()
 
-    def minus(k, f):
+    def times(block, f):
         wide = jnp.broadcast_to(f, (8, PANEL))
 
         def body(i, carry):
             px, py = i // NY, lax.rem(i, NY)
             for h in range(2):
-                prod = G[h, px, py, k] * wide
+                prod = block(px, py, h) * wide
                 part = prod[:, :128] + prod[:, 128:256] + prod[:, 256:384] + prod[:, 384:]
                 PART[pl.ds(pl.multiple_of(i * SHARE + h * HALF, HALF), HALF)] = part
             return carry
@@ -458,10 +521,14 @@
         acc = lax.fori_loop(0, NCOL, body, jnp.zeros((8, PANEL), F32), unroll=8)
         return jnp.sum(acc, axis=0, keepdims=True)
 
-    def solve_first(it, rhs):
+    def forward_of(rhs):
         forward = [rhs[0]]
         for k in range(1, NPANEL):
-            forward.append(rhs[k] - minus(k - 1, forward[-1]))
+            forward.append(rhs[k] - times(lambda px, py, h: G[h, px, py, k - 1], forward[-1]))
+        return forward
+
+    def solve_first(it, rhs):
+        forward = forward_of(rhs)
         rows = []
         for k in range(NPANEL):
             prod = piv[k] * forward[k]
@@ -486,6 +553,9 @@
             ).astype(BF16)
             value = added(dot(got, spread))
             scaled.append(jnp.sum(jnp.where(owner, value, 0.0), axis=0, keepdims=True))
+        return backward_of(scaled)
+
+    def backward_of(scaled):
         ports = [None] * NPANEL
         ports[NPANEL - 1] = scaled[NPANEL - 1]
         for k in range(NPANEL - 2, -1, -1):
@@ -511,6 +581,7 @@
         return jnp.concatenate([jnp.where(lane_row // 32 == min(a, 3), own, 0.0) for a in range(4)], axis=0)
 
     first = solve_first(0, rhs)
+    panel.pass_x(0, 1, 7)
     ports1 = solve_second(0, first)
 
     own_row = c * 4 + r
@@ -557,6 +628,7 @@
         Q[p], T[p], CH[p] = t, t, t
     send_layers(4, [v[p] * T[p] for p in range(2)])
     send_rims(4, [s[p] * T[p] for p in range(2)])
+    panel.pass_x(2, 6, 3, 5, 4)
 
     lifted_map = jnp.zeros((384, 128), F32)
     for k in range(NPANEL):
@@ -594,13 +666,26 @@
     for copy in plane_second:
         copy.wait_recv()
     rhs = select_ports(tile_map(lambda k: X[1, k]) - coarse)
-    second = solve_first(1, rhs)
+    forward = forward_of(rhs)
+    for k in range(NPANEL):
+        FW[k : k + 1] = forward[k]
+    panel.end()
+    SL[l] = times(
+        lambda px, py, h: GP[px, py, HALF * h : HALF * (h + 1)], FW[pl.ds(l, 1)]
+    )
+    second = [
+        remote(SL.at[l], SL.at[l], ls.at[d - 1], lr.at[d - 1], (lax.rem(l + d, 4), r, c)) for d in range(1, 4)
+    ]
+    for copy in second:
+        copy.start()
 
     rho = sweep(4, 1.0 / sigma, s, v)
     send_layers(5, [v[p] * T[p] for p in range(2)])
     send_rims(5, [s[p] * T[p] for p in range(2)])
 
-    ports2 = solve_second(1, second)
+    for copy in second:
+        copy.wait_recv()
+    ports2 = backward_of([SL[k] for k in range(NPANEL)])
     for k in range(NPANEL):
         ports_out[k : k + 1] = ports2[k]
     near = lifted_rows(ports2, [own_row])
@@ -614,14 +699,12 @@
     for rd in range(6):
         left(layer_copies(rd))
         left(rim_copies(rd))
-    for copy in copies_y + group_first + group_coef + group_second:
+    lower.sent()
+    panel.sent()
+    for copy in group_first + group_coef + group_second:
         copy.wait_send()
     for copy in plane_first + plane_coef + plane_second + first + second:
         copy.wait_send()
-    for d in range(NY):
-        for copy in copies_x(d):
-            copy.wait_send()
-        copy_forward(d).wait_send()
     for j in range(NX):
         copy_sibling(j).wait_send()
 
@@ -636,9 +719,14 @@
             jax.ShapeDtypeStruct((2, ROWS, COLS), F32),
             jax.ShapeDtypeStruct((NPANEL, PANEL), F32),
         ),
-        in_specs=[vmem] * 8,
+        in_specs=[pl.BlockSpec(memory_space=pl.ANY)] * 8,
         out_specs=(vmem, vmem),
         scratch_shapes=[
+            field, field, field,
+            pltpu.VMEM((2, ROWS, COLS), jnp.int32),
+            pltpu.VMEM((ROWS, COLS), jnp.int32),
+            pltpu.VMEM((NPANEL, PANEL), jnp.int32),
+            pltpu.VMEM((NPANEL, SHARE, PANEL), F32),
             field, field, field, field, field, field, field, field,
             pltpu.VMEM((6, 2, ROWS, COLS), F32),
             pltpu.VMEM((6, 2, ROWS, COLS), F32),
@@ -647,6 +735,9 @@
             pltpu.VMEM((6, 2, 1, 128), F32),
             pltpu.VMEM((6, 2, 1, 128), F32),
             pltpu.VMEM((2, NX, NY, NPANEL - 1, HALF, PANEL), F32),
+            pltpu.VMEM((NX, NY, SHARE, PANEL), F32),
+            pltpu.VMEM((NPANEL, PANEL), F32),
+            pltpu.VMEM((4, 1, PANEL), F32),
             pltpu.VMEM((PANEL, 128), F32),
             pltpu.VMEM((2, 1, 128), F32),
             pltpu.VMEM((2, 16, 1, 128), F32),
@@ -663,17 +754,21 @@
             pltpu.VMEM((COLS, 128), BF16),
             pltpu.VMEM((8, 128), F32),
             pltpu.VMEM((ROWS, COLS), F32),
-            dma((6, 6)), dma((6, 6)),
+            dma((9,)), dma((6, 6)), dma((6, 6)),
             dma((7,)), dma((7,)),
             dma((2, 8)), dma((2, 8)),
             dma((8,)), dma((8,)),
+            dma((7,)), dma((7,)),
+            dma((2, 8)), dma((2, 8)),
+            dma((8,)), dma((8,)),
+            dma((3,)), dma((3,)),
             dma((4,)), dma((4,)),
             dma((3, 15)), dma((3, 15)),
             dma((3, 31)), dma((3, 31)),
             dma((2, 31)), dma((2, 31)),
         ],
         compiler_params=pltpu.CompilerParams(
-            collective_id=0, has_side_effects=True, vmem_limit_bytes=48 * 1024 * 1024
+            collective_id=0, has_side_effects=True, vmem_limit_bytes=60 * 1024 * 1024
         ),
         cost_estimate=pl.CostEstimate(flops=100_000_000, bytes_accessed=2_000_000, transcendentals=300_000),
         name="grid",

time: 78.9 us -> 74 us (0.938)
  local copies, waits for them, and re-layouts: 8.49 us -> 2.28 us
  Pallas kernels: 69.4 us -> 71 us
    unnamed x18 -> x4, local copies, waits for them, and re-layouts: 8.49 us -> 2.28 us
    pallas_call x1, Pallas kernels: 69.4 us -> 71 us  [shards(): pl.pallas_call(kernel, out_shape=(jax.ShapeDtypeStruct((2, ROWS, COLS), F...]
where the time goes in v2:
time: 74 us; the launch traced here: 73.9 us
  Pallas kernels  71 us (96%)
  local copies, waits for them, and re-layouts  2.28 us (3%)
    pallas_call x1, Pallas kernels, shards(): pl.pallas_call(kernel, out_shape=(jax.ShapeDtypeStruct((2, ROWS, COLS), F...  71 us
    unnamed x4, local copies, waits for them, and re-layouts  2.28 us

profile of v2, /device:TPU:1, one launch (start us, length us, event | category | flops | bytes accessed | tf_op | source)
XLA Modules:
  0.0 73.9 jit_solution(1326442232746274818)
XLA Ops:
  0.6 71.0 %grid.1 = (f32[2,64,512]{2,1,0:T(8,128)}, f32[4,512]{1,0:T(4,128)}) custom-call(f32[2,64,512]{2,1,0:T(8,128)} %src_in.1, f32[2,64,512]{2,1,0:T(8,128)} %cond_in.1, f32[2,64,512]{2,1,0:T(8,128)} %via_in.1, s32[2,64,512]{2,1,0:T(8,128)} %vmap_in.1, s32[64,512]{1,0:T(8,128)} %pad_in.1, s32[4,512]{1,0:T(4,128)} %pt_in.1, f32[4,16,512]{2,1,0:T(8,128)} %piv_in.1, ...), custom_call_target="tpu_custom_call" | custom-call | flops 100000000 | bytes 2000000 | tf_op jit(solution)/shard_map/grid/pallas_call | solution.py:716
  71.6 0.0 copy-start
  71.6 1.7 %copy.12 = f32[2,64,512]{2,1,0:T(8,128)} copy(f32[2,64,512]{2,1,0:T(8,128)} %get-tuple-element.4) | data formatting | bytes 524288
  73.3 0.0 copy-done
  73.3 0.6 copy.13
Async XLA Ops:
  71.6 1.7 %copy-start = (f32[4,512]{1,0:T(4,128)S(1)}, f32[4,512]{1,0:T(4,128)}, u32[]{:S(2)}) copy-start(f32[4,512]{1,0:T(4,128)} %get-tuple-element.5) | copy-start | bytes 24580

commit v3 on v2

--- a/solution.py
+++ b/solution.py
@@ -61,7 +61,7 @@
     drop_out, ports_out,
     src, cond, via, vmap, pad, pt, piv,
     S, V, INV, DP, VS, Q, T, CH, HSEND, HALO, RSEND, RIM, CSEND, SIDE,
-    G, GP, FW, SL, PART, ZSEND, Z, XM, X, CSND, CZ, CXM, CX, SBM, SB, LANES, ROWM, E4, MAPS, LIFT,
+    G, GP, FW, SL, PART, ZSEND, Z, XM, X, CSND, CZ, CXM, CX, SBM, SB, LANES, ROWM, E4,
     ins, hs, hr, gys, gyr, gxs, gxr, gfs, gfr,
     pys, pyr, pxs, pxr, pfs, pfr, ls, lr, gbs, gbr, zs, zr, xs, xr, bs, br,
 ):
@@ -192,11 +192,13 @@
         for p in range(2):
             RSEND[rd, 0, p : p + 1] = g[p][:1]
             RSEND[rd, 1, p : p + 1] = g[p][ROWS - 1 :]
+        copies = rim_copies(rd)
+        start(copies[:2])
         first = jnp.concatenate([g[0][:, :128], g[1][:, :128]], axis=0)
         last = jnp.concatenate([g[0][:, COLS - 128 :], g[1][:, COLS - 128 :]], axis=0)
         CSEND[rd, 0] = first.T[:1]
         CSEND[rd, 1] = last.T[127:]
-        start(rim_copies(rd))
+        start(copies[2:])
 
     def column(rim):
         return jnp.broadcast_to(rim, (128, 128)).T
@@ -363,6 +365,7 @@
 
     lower.pass_y(1, 7)
     lower.send_x(1, 7)
+    lower.pass_x(0)
 
     def gather_plane(it, buf, msg, bufx):
         for q in range(4):
@@ -380,6 +383,39 @@
     for copy in group_first:
         copy.wait_recv()
     plane_first = gather_plane(0, Z.at[0], XM.at[0], X.at[0])
+
+    lower.pass_y(2, 6)
+    lower.send_x(2, 6)
+
+    def sweep(rd, rho, s, v):
+        rho_new = 1.0 / (2.0 * sigma - rho)
+        t = [T[0], T[1]]
+        arrive(rim_copies(rd))
+        around = received_sum(rd, [s[p] * t[p] for p in range(2)])
+        arrive(layer_copies(rd))
+        vert = [HALO[rd, 0] + v[1] * t[1], v[0] * t[0] + HALO[rd, 1]]
+        for p in range(2):
+            remain = Q[p] - t[p] + INV[p] * (s[p] * around[p] + v[p] * vert[p])
+            ch = (rho_new * rho) * CH[p] + (2.0 * rho_new / delta) * remain
+            CH[p] = ch
+            T[p] = t[p] + ch
+        return rho_new
+
+    rho = sweep(1, 1.0 / sigma, s, v)
+    send_layers(2, [v[p] * T[p] for p in range(2)])
+    send_rims(2, [s[p] * T[p] for p in range(2)])
+
+    lower.pass_y(3, 5, 4)
+    lower.send_x(3, 5, 4)
+    lower.pass_x(1, 7)
+    copy_sibling(0).start()
+
+    sweep(2, rho, s, v)
+    send_layers(3, [v[p] * T[p] for p in range(2)])
+    send_rims(3, [s[p] * T[p] for p in range(2)])
+
+    lower.pass_x(2, 6)
+    panel.begin()
 
     west_col, east_col = SIDE[0, 0], SIDE[0, 1]
     east_side = column(east_col)
@@ -397,32 +433,47 @@
     for copy in group_coef:
         copy.start()
 
-    lower.pass_y(2, 6)
-    lower.send_x(2, 6)
-
-    def sweep(rd, rho, s, v):
-        rho_new = 1.0 / (2.0 * sigma - rho)
-        t = [T[0], T[1]]
-        arrive(rim_copies(rd))
-        around = received_sum(rd, [s[p] * t[p] for p in range(2)])
-        arrive(layer_copies(rd))
-        vert = [HALO[rd, 0] + v[1] * t[1], v[0] * t[0] + HALO[rd, 1]]
-        for p in range(2):
-            remain = Q[p] - t[p] + INV[p] * (s[p] * around[p] + v[p] * vert[p])
-            ch = (rho_new * rho) * CH[p] + (2.0 * rho_new / delta) * remain
-            CH[p] = ch
-            T[p] = t[p] + ch
-        return rho_new
-
-    rho = sweep(1, 1.0 / sigma, s, v)
-    send_layers(2, [v[p] * T[p] for p in range(2)])
-    send_rims(2, [s[p] * T[p] for p in range(2)])
-
-    lower.pass_y(3, 5, 4)
-    lower.send_x(3, 5, 4)
-    panel.begin()
-    copy_sibling(0).start()
-
+    def tile_map(load):
+        return jnp.concatenate([load(k) for k in range(NCOL)], axis=0)
+
+    def row_mask(k):
+        return iota((128, PANEL), 0) == ROWM[k : k + 1]
+
+    def select_ports(tiles):
+        parts = stacked(tiles)
+        out = []
+        for k in range(NPANEL):
+            picked = added(dot(parts, LANES[k]))
+            out.append(
+                jnp.sum(jnp.where(row_mask(k), picked, 0.0), axis=0, keepdims=True) * (restrict_scale / TILE)
+            )
+        return out
+
+    for copy in plane_first:
+        copy.wait_recv()
+    rhs = select_ports(tile_map(lambda k: X[0, k]))
+
+    lower.pass_x(3, 5, 4)
+    copy_sibling(1).start()
+    copy_sibling(3).start()
+
+    arrive(rim_copies(3))
+    around = received_sum(3, [s[p] * T[p] for p in range(2)])
+    flat = [src[p] - (DP[p] * T[p] - s[p] * around[p]) for p in range(2)]
+    ZSEND[1] = tile_row(flat[0] + flat[1])
+    Z[1, r * 4 + l] = ZSEND[1]
+    group_second = group_copies(2, 1, Z.at[1], ZSEND.at[1])
+    for copy in group_second:
+        copy.start()
+
+    arrive(layer_copies(3))
+    vert = [HALO[3, 0] + v[1] * T[1], v[0] * T[0] + HALO[3, 1]]
+    for p in range(2):
+        t = T[p]
+        Q[p] = flat[p] - v[p] * (VS[p] * t - vert[p])
+    lower.end()
+    copy_sibling(2).start()
+    panel.pass_y(1, 7, 2, 6)
     for copy in group_coef:
         copy.wait_recv()
     for q in range(4):
@@ -436,58 +487,6 @@
     for copy in plane_coef:
         copy.start()
 
-    sweep(2, rho, s, v)
-    send_layers(3, [v[p] * T[p] for p in range(2)])
-    send_rims(3, [s[p] * T[p] for p in range(2)])
-
-    lower.pass_x(0, 1, 7)
-    panel.pass_y(1, 7)
-
-    def tile_map(load):
-        return jnp.concatenate([load(k) for k in range(NCOL)], axis=0)
-
-    def row_mask(k):
-        return iota((128, PANEL), 0) == ROWM[k : k + 1]
-
-    def select_ports(tiles):
-        parts = stacked(tiles)
-        out = []
-        for k in range(NPANEL):
-            picked = added(dot(parts, LANES[k]))
-            out.append(
-                jnp.sum(jnp.where(row_mask(k), picked, 0.0), axis=0, keepdims=True) * (restrict_scale / TILE)
-            )
-        return out
-
-    for copy in plane_first:
-        copy.wait_recv()
-    rhs = select_ports(tile_map(lambda k: X[0, k]))
-
-    arrive(rim_copies(3))
-    arrive(layer_copies(3))
-    around = received_sum(3, [s[p] * T[p] for p in range(2)])
-    vert = [HALO[3, 0] + v[1] * T[1], v[0] * T[0] + HALO[3, 1]]
-    for p in range(2):
-        t = T[p]
-        Q[p] = src[p] - ((DP[p] + v[p] * VS[p]) * t - s[p] * around[p] - v[p] * vert[p])
-    ZSEND[1] = tile_row(Q[0] + Q[1])
-    Z[1, r * 4 + l] = ZSEND[1]
-    group_second = group_copies(2, 1, Z.at[1], ZSEND.at[1])
-    for copy in group_second:
-        copy.start()
-
-    lower.pass_x(2, 6, 3, 5, 4)
-    panel.pass_y(2, 6)
-    copy_sibling(1).start()
-    copy_sibling(3).start()
-    for copy in group_second:
-        copy.wait_recv()
-    plane_second = gather_plane(2, Z.at[1], XM.at[1], X.at[1])
-    lower.end()
-    copy_sibling(2).start()
-    panel.send_x(0, 1, 7, 2, 6)
-    panel.pass_y(3, 5, 4)
-    panel.send_x(3, 5, 4)
     for j in range(NX):
         copy_sibling(j).wait_recv()
 
@@ -581,7 +580,11 @@
         return jnp.concatenate([jnp.where(lane_row // 32 == min(a, 3), own, 0.0) for a in range(4)], axis=0)
 
     first = solve_first(0, rhs)
-    panel.pass_x(0, 1, 7)
+    for copy in group_second:
+        copy.wait_recv()
+    plane_second = gather_plane(2, Z.at[1], XM.at[1], X.at[1])
+    panel.pass_y(3, 5, 4)
+    panel.send_x(0, 1, 7, 2, 6, 3, 5, 4)
     ports1 = solve_second(0, first)
 
     own_row = c * 4 + r
@@ -607,7 +610,6 @@
     lift = jnp.concatenate(
         [jnp.broadcast_to(level[a : a + 1], (TILE, COLS)) for a in range(4)], axis=0
     )
-    LIFT[...] = lift
     at_row = lax.rem(iota((128, 128), 1), ROWS) // TILE * 32
     pick_w = jnp.where(iota((128, 128), 0) == at_row + 31, 1.0, 0.0).astype(BF16)
     pick_e = jnp.where(iota((128, 128), 0) == at_row, 1.0, 0.0).astype(BF16)
@@ -628,7 +630,7 @@
         Q[p], T[p], CH[p] = t, t, t
     send_layers(4, [v[p] * T[p] for p in range(2)])
     send_rims(4, [s[p] * T[p] for p in range(2)])
-    panel.pass_x(2, 6, 3, 5, 4)
+    panel.pass_x(0, 1, 7, 2, 6, 3, 5, 4)
 
     lifted_map = jnp.zeros((384, 128), F32)
     for k in range(NPANEL):
@@ -752,8 +754,6 @@
             pltpu.VMEM((NPANEL, 128, PANEL), BF16),
             pltpu.VMEM((NPANEL, PANEL), jnp.int32),
             pltpu.VMEM((COLS, 128), BF16),
-            pltpu.VMEM((8, 128), F32),
-            pltpu.VMEM((ROWS, COLS), F32),
             dma((9,)), dma((6, 6)), dma((6, 6)),
             dma((7,)), dma((7,)),
             dma((2, 8)), dma((2, 8)),

time: 74 us -> 71.2 us (0.962)
  Pallas kernels: 71 us -> 68.2 us
    pallas_call x1, Pallas kernels: 71 us -> 68.2 us  [shards(): pl.pallas_call(kernel, out_shape=(jax.ShapeDtypeStruct((2, ROWS, COLS), F...]
where the time goes in v3:
time: 71.2 us; the launch traced here: 71.1 us
  Pallas kernels  68.2 us (96%)
  local copies, waits for them, and re-layouts  2.28 us (3%)
    pallas_call x1, Pallas kernels, shards(): pl.pallas_call(kernel, out_shape=(jax.ShapeDtypeStruct((2, ROWS, COLS), F...  68.2 us
    unnamed x4, local copies, waits for them, and re-layouts  2.28 us

profile of v3, /device:TPU:1, one launch (start us, length us, event | category | flops | bytes accessed | tf_op | source)
XLA Modules:
  0.0 71.1 jit_solution(1861667378216577257)
XLA Ops:
  0.6 68.2 %grid.1 = (f32[2,64,512]{2,1,0:T(8,128)}, f32[4,512]{1,0:T(4,128)}) custom-call(f32[2,64,512]{2,1,0:T(8,128)} %src_in.1, f32[2,64,512]{2,1,0:T(8,128)} %cond_in.1, f32[2,64,512]{2,1,0:T(8,128)} %via_in.1, s32[2,64,512]{2,1,0:T(8,128)} %vmap_in.1, s32[64,512]{1,0:T(8,128)} %pad_in.1, s32[4,512]{1,0:T(4,128)} %pt_in.1, f32[4,16,512]{2,1,0:T(8,128)} %piv_in.1, ...), custom_call_target="tpu_custom_call" | custom-call | flops 100000000 | bytes 2000000 | tf_op jit(solution)/shard_map/grid/pallas_call | solution.py:718
  68.8 0.0 copy-start
  68.8 1.7 %copy.12 = f32[2,64,512]{2,1,0:T(8,128)} copy(f32[2,64,512]{2,1,0:T(8,128)} %get-tuple-element.4) | data formatting | bytes 524288
  70.5 0.0 copy-done
  70.5 0.6 copy.13
Async XLA Ops:
  68.8 1.7 %copy-start = (f32[4,512]{1,0:T(4,128)S(1)}, f32[4,512]{1,0:T(4,128)}, u32[]{:S(2)}) copy-start(f32[4,512]{1,0:T(4,128)} %get-tuple-element.5) | copy-start | bytes 24580

commit v4 on v3

--- a/solution.py
+++ b/solution.py
@@ -72,12 +72,21 @@
     def at_col(px, py):
         return (l, r, px * NY + py)
 
-    group = [(lax.rem(l + d % 4, 4), lax.rem(r + d // 4, 4), c) for d in range(1, 16)]
-    plane_peers = [(l, r, lax.rem(c + d, NCOL)) for d in range(1, NCOL)]
+    def far(d, n, m):
+        i, j = d // m, d % m
+        return -(min(i, n - i) + min(j, m - j))
+
+    group = [
+        (lax.rem(l + d % 4, 4), lax.rem(r + d // 4, 4), c)
+        for d in sorted(range(1, 16), key=lambda d: far(d, 4, 4) - min(d // 4, 4 - d // 4))
+    ]
+    plane_peers = [
+        (l, r, lax.rem(c + d, NCOL)) for d in sorted(range(1, NCOL), key=lambda d: far(d, NX, NY))
+    ]
     sibling = (l + 1 - 2 * core, r, c)
 
     barrier = pltpu.get_barrier_semaphore()
-    for peer in group + plane_peers:
+    for peer in plane_peers + group:
         pl.semaphore_signal(barrier, inc=1, device_id=peer, device_id_type=MESH)
 
     def remote(a, b, ssem, rsem, peer):
@@ -345,8 +354,10 @@
         LANES[k] = jnp.where(iota((128, PANEL), 0) == lane, 1.0, 0.0).astype(BF16)
         ROWM[k : k + 1] = (acol // 32) * 4 + arow // 4
 
+    arrive(rim_copies(0))
+    lower.pass_y(1, 7)
+    lower.send_x(1, 7)
     arrive(layer_copies(0))
-    arrive(rim_copies(0))
     s = [S[0], S[1]]
     v = [V[0], V[1]]
     around = received_sum(0, s)
@@ -363,9 +374,8 @@
     send_layers(1, [v[p] * T[p] for p in range(2)])
     send_rims(1, [s[p] * T[p] for p in range(2)])
 
-    lower.pass_y(1, 7)
-    lower.send_x(1, 7)
-    lower.pass_x(0)
+    lower.pass_y(2, 6)
+    lower.send_x(2, 6)
 
     def gather_plane(it, buf, msg, bufx):
         for q in range(4):
@@ -384,8 +394,9 @@
         copy.wait_recv()
     plane_first = gather_plane(0, Z.at[0], XM.at[0], X.at[0])
 
-    lower.pass_y(2, 6)
-    lower.send_x(2, 6)
+    lower.pass_x(0)
+    lower.pass_y(3, 5, 4)
+    lower.send_x(3, 5, 4)
 
     def sweep(rd, rho, s, v):
         rho_new = 1.0 / (2.0 * sigma - rho)
@@ -405,16 +416,16 @@
     send_layers(2, [v[p] * T[p] for p in range(2)])
     send_rims(2, [s[p] * T[p] for p in range(2)])
 
-    lower.pass_y(3, 5, 4)
-    lower.send_x(3, 5, 4)
-    lower.pass_x(1, 7)
+    lower.pass_x(1, 7, 2, 6)
     copy_sibling(0).start()
 
     sweep(2, rho, s, v)
     send_layers(3, [v[p] * T[p] for p in range(2)])
     send_rims(3, [s[p] * T[p] for p in range(2)])
 
-    lower.pass_x(2, 6)
+    lower.pass_x(3, 5, 4)
+    copy_sibling(1).start()
+    copy_sibling(3).start()
     panel.begin()
 
     west_col, east_col = SIDE[0, 0], SIDE[0, 1]
@@ -453,9 +464,9 @@
         copy.wait_recv()
     rhs = select_ports(tile_map(lambda k: X[0, k]))
 
-    lower.pass_x(3, 5, 4)
-    copy_sibling(1).start()
-    copy_sibling(3).start()
+    lower.end()
+    copy_sibling(2).start()
+    panel.pass_y(1, 7, 2, 6)
 
     arrive(rim_copies(3))
     around = received_sum(3, [s[p] * T[p] for p in range(2)])
@@ -465,30 +476,6 @@
     group_second = group_copies(2, 1, Z.at[1], ZSEND.at[1])
     for copy in group_second:
         copy.start()
-
-    arrive(layer_copies(3))
-    vert = [HALO[3, 0] + v[1] * T[1], v[0] * T[0] + HALO[3, 1]]
-    for p in range(2):
-        t = T[p]
-        Q[p] = flat[p] - v[p] * (VS[p] * t - vert[p])
-    lower.end()
-    copy_sibling(2).start()
-    panel.pass_y(1, 7, 2, 6)
-    for copy in group_coef:
-        copy.wait_recv()
-    for q in range(4):
-        total = CZ[4 * q]
-        for k in range(1, 4):
-            total = total + CZ[4 * q + k]
-        for k in range(3):
-            CXM[k, q : q + 1] = total[k : k + 1]
-    CX[c] = CXM[...]
-    plane_coef = plane_copies(1, CXM, CX, xs, xr)
-    for copy in plane_coef:
-        copy.start()
-
-    for j in range(NX):
-        copy_sibling(j).wait_recv()
 
     def times(block, f):
         wide = jnp.broadcast_to(f, (8, PANEL))
@@ -579,7 +566,29 @@
     def field_of(own):
         return jnp.concatenate([jnp.where(lane_row // 32 == min(a, 3), own, 0.0) for a in range(4)], axis=0)
 
+    for j in range(NX):
+        copy_sibling(j).wait_recv()
     first = solve_first(0, rhs)
+
+    arrive(layer_copies(3))
+    vert = [HALO[3, 0] + v[1] * T[1], v[0] * T[0] + HALO[3, 1]]
+    for p in range(2):
+        t = T[p]
+        Q[p] = flat[p] - v[p] * (VS[p] * t - vert[p])
+    for copy in group_coef:
+        copy.wait_recv()
+    for q in range(4):
+        total = CZ[4 * q]
+        for k in range(1, 4):
+            total = total + CZ[4 * q + k]
+        for k in range(3):
+            CXM[k, q : q + 1] = total[k : k + 1]
+    CX[c] = CXM[...]
+    plane_coef = plane_copies(1, CXM, CX, xs, xr)
+    for copy in plane_coef:
+        copy.start()
+
+
     for copy in group_second:
         copy.wait_recv()
     plane_second = gather_plane(2, Z.at[1], XM.at[1], X.at[1])
@@ -630,7 +639,7 @@
         Q[p], T[p], CH[p] = t, t, t
     send_layers(4, [v[p] * T[p] for p in range(2)])
     send_rims(4, [s[p] * T[p] for p in range(2)])
-    panel.pass_x(0, 1, 7, 2, 6, 3, 5, 4)
+    panel.pass_x(0, 1, 7, 2, 6)
 
     lifted_map = jnp.zeros((384, 128), F32)
     for k in range(NPANEL):
@@ -665,9 +674,14 @@
     flow_s = edge_s * (lifted_map - tile_south(lifted_map))
     coarse = pads_map * lifted_map + flow_e - tile_west(flow_e) + flow_s - tile_north(flow_s)
 
+    panel.pass_x(3, 5, 4)
     for copy in plane_second:
         copy.wait_recv()
     rhs = select_ports(tile_map(lambda k: X[1, k]) - coarse)
+    rho = sweep(4, 1.0 / sigma, s, v)
+    send_layers(5, [v[p] * T[p] for p in range(2)])
+    send_rims(5, [s[p] * T[p] for p in range(2)])
+
     forward = forward_of(rhs)
     for k in range(NPANEL):
         FW[k : k + 1] = forward[k]
@@ -680,10 +694,6 @@
     ]
     for copy in second:
         copy.start()
-
-    rho = sweep(4, 1.0 / sigma, s, v)
-    send_layers(5, [v[p] * T[p] for p in range(2)])
-    send_rims(5, [s[p] * T[p] for p in range(2)])
 
     for copy in second:
         copy.wait_recv()

time: 71.2 us -> 72.1 us (1.013)
  Pallas kernels: 68.2 us -> 69 us
    pallas_call x1, Pallas kernels: 68.2 us -> 69 us  [shards(): pl.pallas_call(kernel, out_shape=(jax.ShapeDtypeStruct((2, ROWS, COLS), F...]
where the time goes in v4:
time: 72.1 us; the launch traced here: 72 us
  Pallas kernels  69 us (96%)
  local copies, waits for them, and re-layouts  2.28 us (3%)
    pallas_call x1, Pallas kernels, shards(): pl.pallas_call(kernel, out_shape=(jax.ShapeDtypeStruct((2, ROWS, COLS), F...  69 us
    unnamed x4, local copies, waits for them, and re-layouts  2.28 us

profile of v4, /device:TPU:1, one launch (start us, length us, event | category | flops | bytes accessed | tf_op | source)
XLA Modules:
  0.0 72.0 jit_solution(12970226035643817100)
XLA Ops:
  0.6 69.0 %grid.1 = (f32[2,64,512]{2,1,0:T(8,128)}, f32[4,512]{1,0:T(4,128)}) custom-call(f32[2,64,512]{2,1,0:T(8,128)} %src_in.1, f32[2,64,512]{2,1,0:T(8,128)} %cond_in.1, f32[2,64,512]{2,1,0:T(8,128)} %via_in.1, s32[2,64,512]{2,1,0:T(8,128)} %vmap_in.1, s32[64,512]{1,0:T(8,128)} %pad_in.1, s32[4,512]{1,0:T(4,128)} %pt_in.1, f32[4,16,512]{2,1,0:T(8,128)} %piv_in.1, ...), custom_call_target="tpu_custom_call" | custom-call | flops 100000000 | bytes 2000000 | tf_op jit(solution)/shard_map/grid/pallas_call | solution.py:728
  69.7 0.0 copy-start
  69.7 1.7 %copy.12 = f32[2,64,512]{2,1,0:T(8,128)} copy(f32[2,64,512]{2,1,0:T(8,128)} %get-tuple-element.4) | data formatting | bytes 524288
  71.4 0.0 copy-done
  71.4 0.6 copy.13
Async XLA Ops:
  69.7 1.7 %copy-start = (f32[4,512]{1,0:T(4,128)S(1)}, f32[4,512]{1,0:T(4,128)}, u32[]{:S(2)}) copy-start(f32[4,512]{1,0:T(4,128)} %get-tuple-element.5) | copy-start | bytes 24580

commit v5 on v4

--- a/solution.py
+++ b/solution.py
@@ -192,22 +192,20 @@
             def _():
                 copy.wait_send()
 
-    def send_layers(rd, h):
+    def send_round(rd, g, h):
+        rims = rim_copies(rd)
+        for p in range(2):
+            RSEND[rd, 0, p : p + 1] = g[p][:1]
+            RSEND[rd, 1, p : p + 1] = g[p][ROWS - 1 :]
+        start(rims[:2])
         for p in range(2):
             HSEND[rd, p] = h[p]
         start(layer_copies(rd))
-
-    def send_rims(rd, g):
-        for p in range(2):
-            RSEND[rd, 0, p : p + 1] = g[p][:1]
-            RSEND[rd, 1, p : p + 1] = g[p][ROWS - 1 :]
-        copies = rim_copies(rd)
-        start(copies[:2])
         first = jnp.concatenate([g[0][:, :128], g[1][:, :128]], axis=0)
         last = jnp.concatenate([g[0][:, COLS - 128 :], g[1][:, COLS - 128 :]], axis=0)
         CSEND[rd, 0] = first.T[:1]
         CSEND[rd, 1] = last.T[127:]
-        start(copies[2:])
+        start(rims[2:])
 
     def column(rim):
         return jnp.broadcast_to(rim, (128, 128)).T
@@ -266,8 +264,7 @@
 
     pl.semaphore_wait(barrier, 15 + 31)
 
-    send_layers(0, [V[0], V[1]])
-    send_rims(0, [S[0], S[1]])
+    send_round(0, [S[0], S[1]], [V[0], V[1]])
 
     turn = 1 - 2 * core
 
@@ -371,8 +368,7 @@
         inv = 1.0 / (dp + v[p] * vsum[p])
         t = inv * src[p]
         DP[p], INV[p], VS[p], Q[p], T[p], CH[p] = dp, inv, vsum[p], t, t, t
-    send_layers(1, [v[p] * T[p] for p in range(2)])
-    send_rims(1, [s[p] * T[p] for p in range(2)])
+    send_round(1, [s[p] * T[p] for p in range(2)], [v[p] * T[p] for p in range(2)])
 
     lower.pass_y(2, 6)
     lower.send_x(2, 6)
@@ -394,9 +390,9 @@
         copy.wait_recv()
     plane_first = gather_plane(0, Z.at[0], XM.at[0], X.at[0])
 
-    lower.pass_x(0)
     lower.pass_y(3, 5, 4)
     lower.send_x(3, 5, 4)
+    lower.pass_x(0, 1, 7)
 
     def sweep(rd, rho, s, v):
         rho_new = 1.0 / (2.0 * sigma - rho)
@@ -413,15 +409,13 @@
         return rho_new
 
     rho = sweep(1, 1.0 / sigma, s, v)
-    send_layers(2, [v[p] * T[p] for p in range(2)])
-    send_rims(2, [s[p] * T[p] for p in range(2)])
-
-    lower.pass_x(1, 7, 2, 6)
+    send_round(2, [s[p] * T[p] for p in range(2)], [v[p] * T[p] for p in range(2)])
+
+    lower.pass_x(2, 6)
     copy_sibling(0).start()
 
     sweep(2, rho, s, v)
-    send_layers(3, [v[p] * T[p] for p in range(2)])
-    send_rims(3, [s[p] * T[p] for p in range(2)])
+    send_round(3, [s[p] * T[p] for p in range(2)], [v[p] * T[p] for p in range(2)])
 
     lower.pass_x(3, 5, 4)
     copy_sibling(1).start()
@@ -488,7 +482,7 @@
                 PART[pl.ds(pl.multiple_of(i * SHARE + h * HALF, HALF), HALF)] = part
             return carry
 
-        lax.fori_loop(0, NCOL, body, 0, unroll=8)
+        lax.fori_loop(0, NCOL, body, 0, unroll=NCOL)
         return jnp.concatenate(
             [jnp.sum(PART[128 * j : 128 * (j + 1)].T, axis=0, keepdims=True) for j in range(4)], axis=1
         )
@@ -504,7 +498,7 @@
                 acc = acc + G[h, px, py, k] * jnp.concatenate([w] * 4, axis=1)
             return acc
 
-        acc = lax.fori_loop(0, NCOL, body, jnp.zeros((8, PANEL), F32), unroll=8)
+        acc = lax.fori_loop(0, NCOL, body, jnp.zeros((8, PANEL), F32), unroll=NCOL)
         return jnp.sum(acc, axis=0, keepdims=True)
 
     def forward_of(rhs):
@@ -637,8 +631,7 @@
         t = INV[p] * resid
         drop_out[p] = lift + t3
         Q[p], T[p], CH[p] = t, t, t
-    send_layers(4, [v[p] * T[p] for p in range(2)])
-    send_rims(4, [s[p] * T[p] for p in range(2)])
+    send_round(4, [s[p] * T[p] for p in range(2)], [v[p] * T[p] for p in range(2)])
     panel.pass_x(0, 1, 7, 2, 6)
 
     lifted_map = jnp.zeros((384, 128), F32)
@@ -679,8 +672,7 @@
         copy.wait_recv()
     rhs = select_ports(tile_map(lambda k: X[1, k]) - coarse)
     rho = sweep(4, 1.0 / sigma, s, v)
-    send_layers(5, [v[p] * T[p] for p in range(2)])
-    send_rims(5, [s[p] * T[p] for p in range(2)])
+    send_round(5, [s[p] * T[p] for p in range(2)], [v[p] * T[p] for p in range(2)])
 
     forward = forward_of(rhs)
     for k in range(NPANEL):

time: 72.1 us -> 69.9 us (0.969)
  Pallas kernels: 69 us -> 66.8 us
    pallas_call x1, Pallas kernels: 69 us -> 66.8 us  [shards(): pl.pallas_call(kernel, out_shape=(jax.ShapeDtypeStruct((2, ROWS, COLS), F...]
where the time goes in v5:
time: 69.9 us; the launch traced here: 69.7 us
  Pallas kernels  66.8 us (96%)
  local copies, waits for them, and re-layouts  2.28 us (3%)
    pallas_call x1, Pallas kernels, shards(): pl.pallas_call(kernel, out_shape=(jax.ShapeDtypeStruct((2, ROWS, COLS), F...  66.8 us
    unnamed x4, local copies, waits for them, and re-layouts  2.28 us

profile of v5, /device:TPU:1, one launch (start us, length us, event | category | flops | bytes accessed | tf_op | source)
XLA Modules:
  0.0 69.7 jit_solution(6541472534076469110)
XLA Ops:
  0.6 66.8 %grid.1 = (f32[2,64,512]{2,1,0:T(8,128)}, f32[4,512]{1,0:T(4,128)}) custom-call(f32[2,64,512]{2,1,0:T(8,128)} %src_in.1, f32[2,64,512]{2,1,0:T(8,128)} %cond_in.1, f32[2,64,512]{2,1,0:T(8,128)} %via_in.1, s32[2,64,512]{2,1,0:T(8,128)} %vmap_in.1, s32[64,512]{1,0:T(8,128)} %pad_in.1, s32[4,512]{1,0:T(4,128)} %pt_in.1, f32[4,16,512]{2,1,0:T(8,128)} %piv_in.1, ...), custom_call_target="tpu_custom_call" | custom-call | flops 100000000 | bytes 2000000 | tf_op jit(solution)/shard_map/grid/pallas_call | solution.py:720
  67.4 0.0 copy-start
  67.4 1.7 %copy.12 = f32[2,64,512]{2,1,0:T(8,128)} copy(f32[2,64,512]{2,1,0:T(8,128)} %get-tuple-element.4) | data formatting | bytes 524288
  69.1 0.0 copy-done
  69.1 0.6 copy.13
Async XLA Ops:
  67.4 1.7 %copy-start = (f32[4,512]{1,0:T(4,128)S(1)}, f32[4,512]{1,0:T(4,128)}, u32[]{:S(2)}) copy-start(f32[4,512]{1,0:T(4,128)} %get-tuple-element.5) | copy-start | bytes 24580

commit v6 on v5

--- a/solution.py
+++ b/solution.py
@@ -390,38 +390,6 @@
         copy.wait_recv()
     plane_first = gather_plane(0, Z.at[0], XM.at[0], X.at[0])
 
-    lower.pass_y(3, 5, 4)
-    lower.send_x(3, 5, 4)
-    lower.pass_x(0, 1, 7)
-
-    def sweep(rd, rho, s, v):
-        rho_new = 1.0 / (2.0 * sigma - rho)
-        t = [T[0], T[1]]
-        arrive(rim_copies(rd))
-        around = received_sum(rd, [s[p] * t[p] for p in range(2)])
-        arrive(layer_copies(rd))
-        vert = [HALO[rd, 0] + v[1] * t[1], v[0] * t[0] + HALO[rd, 1]]
-        for p in range(2):
-            remain = Q[p] - t[p] + INV[p] * (s[p] * around[p] + v[p] * vert[p])
-            ch = (rho_new * rho) * CH[p] + (2.0 * rho_new / delta) * remain
-            CH[p] = ch
-            T[p] = t[p] + ch
-        return rho_new
-
-    rho = sweep(1, 1.0 / sigma, s, v)
-    send_round(2, [s[p] * T[p] for p in range(2)], [v[p] * T[p] for p in range(2)])
-
-    lower.pass_x(2, 6)
-    copy_sibling(0).start()
-
-    sweep(2, rho, s, v)
-    send_round(3, [s[p] * T[p] for p in range(2)], [v[p] * T[p] for p in range(2)])
-
-    lower.pass_x(3, 5, 4)
-    copy_sibling(1).start()
-    copy_sibling(3).start()
-    panel.begin()
-
     west_col, east_col = SIDE[0, 0], SIDE[0, 1]
     east_side = column(east_col)
     edge_e = jnp.zeros((ROWS, COLS), F32)
@@ -438,6 +406,51 @@
     for copy in group_coef:
         copy.start()
 
+
+    lower.pass_y(3, 5, 4)
+    lower.send_x(3, 5, 4)
+    lower.pass_x(0, 1, 7)
+
+    def sweep(rd, rho, s, v):
+        rho_new = 1.0 / (2.0 * sigma - rho)
+        t = [T[0], T[1]]
+        arrive(rim_copies(rd))
+        around = received_sum(rd, [s[p] * t[p] for p in range(2)])
+        arrive(layer_copies(rd))
+        vert = [HALO[rd, 0] + v[1] * t[1], v[0] * t[0] + HALO[rd, 1]]
+        for p in range(2):
+            remain = Q[p] - t[p] + INV[p] * (s[p] * around[p] + v[p] * vert[p])
+            ch = (rho_new * rho) * CH[p] + (2.0 * rho_new / delta) * remain
+            CH[p] = ch
+            T[p] = t[p] + ch
+        return rho_new
+
+    rho = sweep(1, 1.0 / sigma, s, v)
+    send_round(2, [s[p] * T[p] for p in range(2)], [v[p] * T[p] for p in range(2)])
+
+    lower.pass_x(2, 6)
+    copy_sibling(0).start()
+    for copy in group_coef:
+        copy.wait_recv()
+    for q in range(4):
+        total = CZ[4 * q]
+        for k in range(1, 4):
+            total = total + CZ[4 * q + k]
+        for k in range(3):
+            CXM[k, q : q + 1] = total[k : k + 1]
+    CX[c] = CXM[...]
+    plane_coef = plane_copies(1, CXM, CX, xs, xr)
+    for copy in plane_coef:
+        copy.start()
+
+    sweep(2, rho, s, v)
+    send_round(3, [s[p] * T[p] for p in range(2)], [v[p] * T[p] for p in range(2)])
+
+    lower.pass_x(3, 5, 4)
+    copy_sibling(1).start()
+    copy_sibling(3).start()
+    panel.begin()
+
     def tile_map(load):
         return jnp.concatenate([load(k) for k in range(NCOL)], axis=0)
 
@@ -569,20 +582,6 @@
     for p in range(2):
         t = T[p]
         Q[p] = flat[p] - v[p] * (VS[p] * t - vert[p])
-    for copy in group_coef:
-        copy.wait_recv()
-    for q in range(4):
-        total = CZ[4 * q]
-        for k in range(1, 4):
-            total = total + CZ[4 * q + k]
-        for k in range(3):
-            CXM[k, q : q + 1] = total[k : k + 1]
-    CX[c] = CXM[...]
-    plane_coef = plane_copies(1, CXM, CX, xs, xr)
-    for copy in plane_coef:
-        copy.start()
-
-
     for copy in group_second:
         copy.wait_recv()
     plane_second = gather_plane(2, Z.at[1], XM.at[1], X.at[1])
@@ -687,6 +686,17 @@
     for copy in second:
         copy.start()
 
+    for rd in range(5):
+        left(layer_copies(rd))
+        left(rim_copies(rd))
+    lower.sent()
+    panel.sent()
+    for copy in group_first + group_coef + group_second:
+        copy.wait_send()
+    for copy in plane_first + plane_coef + plane_second + first:
+        copy.wait_send()
+    for j in range(NX):
+        copy_sibling(j).wait_send()
     for copy in second:
         copy.wait_recv()
     ports2 = backward_of([SL[k] for k in range(NPANEL)])
@@ -700,17 +710,10 @@
             rows = slice(TILE * a, TILE * (a + 1))
             drop_out[p, rows] = drop_out[p, rows] + T[p, rows] + level[a : a + 1]
 
-    for rd in range(6):
-        left(layer_copies(rd))
-        left(rim_copies(rd))
-    lower.sent()
-    panel.sent()
-    for copy in group_first + group_coef + group_second:
+    left(layer_copies(5))
+    left(rim_copies(5))
+    for copy in second:
         copy.wait_send()
-    for copy in plane_first + plane_coef + plane_second + first + second:
-        copy.wait_send()
-    for j in range(NX):
-        copy_sibling(j).wait_send()
 
 
 def shards(*args):

time: 69.9 us -> 70.9 us (1.014)
  Pallas kernels: 66.8 us -> 67.8 us
    pallas_call x1, Pallas kernels: 66.8 us -> 67.8 us  [shards(): pl.pallas_call(kernel, out_shape=(jax.ShapeDtypeStruct((2, ROWS, COLS), F...]
where the time goes in v6:
time: 70.9 us; the launch traced here: 70.8 us
  Pallas kernels  67.8 us (96%)
  local copies, waits for them, and re-layouts  2.28 us (3%)
    pallas_call x1, Pallas kernels, shards(): pl.pallas_call(kernel, out_shape=(jax.ShapeDtypeStruct((2, ROWS, COLS), F...  67.8 us
    unnamed x4, local copies, waits for them, and re-layouts  2.28 us

profile of v6, /device:TPU:1, one launch (start us, length us, event | category | flops | bytes accessed | tf_op | source)
XLA Modules:
  0.0 70.8 jit_solution(831704734749262771)
XLA Ops:
  0.6 67.8 %grid.1 = (f32[2,64,512]{2,1,0:T(8,128)}, f32[4,512]{1,0:T(4,128)}) custom-call(f32[2,64,512]{2,1,0:T(8,128)} %src_in.1, f32[2,64,512]{2,1,0:T(8,128)} %cond_in.1, f32[2,64,512]{2,1,0:T(8,128)} %via_in.1, s32[2,64,512]{2,1,0:T(8,128)} %vmap_in.1, s32[64,512]{1,0:T(8,128)} %pad_in.1, s32[4,512]{1,0:T(4,128)} %pt_in.1, f32[4,16,512]{2,1,0:T(8,128)} %piv_in.1, ...), custom_call_target="tpu_custom_call" | custom-call | flops 100000000 | bytes 2000000 | tf_op jit(solution)/shard_map/grid/pallas_call | solution.py:723
  68.5 0.0 copy-start
  68.5 1.7 %copy.12 = f32[2,64,512]{2,1,0:T(8,128)} copy(f32[2,64,512]{2,1,0:T(8,128)} %get-tuple-element.4) | data formatting | bytes 524288
  70.2 0.0 copy-done
  70.2 0.6 copy.13
Async XLA Ops:
  68.5 1.7 %copy-start = (f32[4,512]{1,0:T(4,128)S(1)}, f32[4,512]{1,0:T(4,128)}, u32[]{:S(2)}) copy-start(f32[4,512]{1,0:T(4,128)} %get-tuple-element.5) | copy-start | bytes 24580

commit v7 on v6

--- a/solution.py
+++ b/solution.py
@@ -442,13 +442,13 @@
     plane_coef = plane_copies(1, CXM, CX, xs, xr)
     for copy in plane_coef:
         copy.start()
-
-    sweep(2, rho, s, v)
-    send_round(3, [s[p] * T[p] for p in range(2)], [v[p] * T[p] for p in range(2)])
-
     lower.pass_x(3, 5, 4)
     copy_sibling(1).start()
     copy_sibling(3).start()
+
+    sweep(2, rho, s, v)
+    send_round(3, [s[p] * T[p] for p in range(2)], [v[p] * T[p] for p in range(2)])
+
     panel.begin()
 
     def tile_map(load):

time: 70.9 us -> 71.2 us (level)
  no operation moved by 1% of the time
where the time goes in v7:
time: 71.2 us; the launch traced here: 71 us
  Pallas kernels  68.1 us (96%)
  local copies, waits for them, and re-layouts  2.28 us (3%)
    pallas_call x1, Pallas kernels, shards(): pl.pallas_call(kernel, out_shape=(jax.ShapeDtypeStruct((2, ROWS, COLS), F...  68.1 us
    unnamed x4, local copies, waits for them, and re-layouts  2.28 us

profile of v7, /device:TPU:1, one launch (start us, length us, event | category | flops | bytes accessed | tf_op | source)
XLA Modules:
  0.0 71.0 jit_solution(10432215435734642520)
XLA Ops:
  0.6 68.1 %grid.1 = (f32[2,64,512]{2,1,0:T(8,128)}, f32[4,512]{1,0:T(4,128)}) custom-call(f32[2,64,512]{2,1,0:T(8,128)} %src_in.1, f32[2,64,512]{2,1,0:T(8,128)} %cond_in.1, f32[2,64,512]{2,1,0:T(8,128)} %via_in.1, s32[2,64,512]{2,1,0:T(8,128)} %vmap_in.1, s32[64,512]{1,0:T(8,128)} %pad_in.1, s32[4,512]{1,0:T(4,128)} %pt_in.1, f32[4,16,512]{2,1,0:T(8,128)} %piv_in.1, ...), custom_call_target="tpu_custom_call" | custom-call | flops 100000000 | bytes 2000000 | tf_op jit(solution)/shard_map/grid/pallas_call | solution.py:723
  68.7 0.0 copy-start
  68.7 1.7 %copy.12 = f32[2,64,512]{2,1,0:T(8,128)} copy(f32[2,64,512]{2,1,0:T(8,128)} %get-tuple-element.4) | data formatting | bytes 524288
  70.4 0.0 copy-done
  70.4 0.6 copy.13
Async XLA Ops:
  68.7 1.7 %copy-start = (f32[4,512]{1,0:T(4,128)S(1)}, f32[4,512]{1,0:T(4,128)}, u32[]{:S(2)}) copy-start(f32[4,512]{1,0:T(4,128)} %get-tuple-element.5) | copy-start | bytes 24580
